TPU v7x, 256 devices: a whole 4x4x8 slice. The times are simulated.
256 devices in a mesh: learn: 16 (over x, z_hi), tp: 4 (over y), dp: 4 (over z_lo, core).
Axes of the slice: x: 4, y: 4, z: 8 (z_hi: 4, z_lo: 2; z = z_hi * 2 + z_lo), core: 2. Of those that a mesh axis runs over, the one named last changes fastest.
Arguments:
- features: bfloat16 [32768, 8192], P(('learn', 'dp'), 'tp'), may hold values from -16 to 16
- kv_cotangent: bfloat16 [32768, 2048], P(('learn', 'dp'), 'tp'), may hold values from -0.032958984 to 0.032958984
- master_weight: float32 [8192, 2048], P(('learn', 'dp'), 'tp'), may hold values from -0.0625 to 0.0625
- first_moment: float32 [8192, 2048], P(('learn', 'dp'), 'tp'), may hold values from -1.2 to 1.2
- second_moment: float32 [8192, 2048], P(('learn', 'dp'), 'tp'), may hold values from 0.0001 to 0.01
- decode_inputs: bfloat16 [4, 128, 8192], P(None, ('learn', 'dp')), may hold values from -6 to 6
- queries: bfloat16 [4, 128, 8192], P(None, ('learn', 'dp'), 'tp'), may hold values from -120 to 120
- kv_cache: bfloat16 [2, 128, 8, 4096, 128], P(None, ('learn', 'dp'), 'tp'), may hold values from -6 to 6, as said below
- cache_lengths: int32 [128], P(('learn', 'dp')), may hold values from 1 to 4096, 264192 in all
Outputs:
- master_out: float32 [8192, 2048], P(('learn', 'dp'), 'tp')
- first_out: float32 [8192, 2048], P(('learn', 'dp'), 'tp')
- second_out: float32 [8192, 2048], P(('learn', 'dp'), 'tp')
- new_kv: bfloat16 [4, 128, 2048], P(None, ('learn', 'dp'), 'tp')
- attended: bfloat16 [4, 128, 8192], P(None, ('learn', 'dp'), 'tp')
Inputs may be any that keep to these rules, and one draw needn't show every extreme that they name: `kv_cache`: normal entries; in some draws a cached key at position 1 is close to the key at position 0. `cache_lengths`: some row has exactly 4096 cached tokens.
All inputs are finite; a program needn't handle non-finite values. No bound on the sum of `cache_lengths` on one device may be relied on, other than what follows from the above.
Results may differ from a plain program's by a relative error of at most 0.005.
Values may be sent and summed in bfloat16 or wider, within the bound.
A program may use at most 128 MiB of HBM per device.

v0:
```python
import jax
import jax.numpy as jnp
from jax import lax
from jax.sharding import PartitionSpec as P

learn_rate = 0.005
decay_rate = 0.1
first_fix = 1.0 - 0.9**10
second_fix = 1.0 - 0.999**10


def attend(queries, kv_cache, cache_lengths, new_kv):
    step_count, row_count = (queries.shape[0], queries.shape[1])
    heads_kv, slot_count, head_size = (kv_cache.shape[2], kv_cache.shape[3], kv_cache.shape[4])
    query_heads = queries.reshape(step_count, row_count, heads_kv, -1, head_size)
    recent = new_kv.reshape(step_count, row_count, heads_kv, 2, head_size)
    score_scale = head_size ** (-0.5)
    cached = (
        jnp.einsum(
            "srhgd,rhpd->srhgp", query_heads, kv_cache[0], preferred_element_type=jnp.float32
        )
        * score_scale
    )
    positions = jnp.arange(slot_count, dtype=jnp.int32)
    allowed = positions[None, :] < cache_lengths[:, None]
    cached = jnp.where(allowed[None, :, None, None, :], cached, -jnp.inf)
    fresh = (
        jnp.einsum(
            "srhgd,jrhd->srhgj",
            query_heads,
            recent[:, :, :, 0, :],
            preferred_element_type=jnp.float32,
        )
        * score_scale
    )
    order = jnp.arange(step_count, dtype=jnp.int32)
    causal = order[None, :] <= order[:, None]
    fresh = jnp.where(causal[:, None, None, None, :], fresh, -jnp.inf)
    highest = jnp.maximum(jnp.max(cached, axis=-1), jnp.max(fresh, axis=-1))[..., None]
    cached_exp = jnp.exp(cached - highest)
    fresh_exp = jnp.exp(fresh - highest)
    denominator = jnp.sum(cached_exp, axis=-1, keepdims=True) + jnp.sum(
        fresh_exp, axis=-1, keepdims=True
    )
    cached_weight = (cached_exp / denominator).astype(jnp.bfloat16)
    fresh_weight = (fresh_exp / denominator).astype(jnp.bfloat16)
    result = jnp.einsum(
        "srhgp,rhpd->srhgd", cached_weight, kv_cache[1], preferred_element_type=jnp.float32
    )
    result = result + jnp.einsum(
        "srhgj,jrhd->srhgd", fresh_weight, recent[:, :, :, 1, :], preferred_element_type=jnp.float32
    )
    return result.reshape(step_count, row_count, -1).astype(jnp.bfloat16)


def shards(
    features,
    kv_cotangent,
    master_weight,
    first_moment,
    second_moment,
    decode_inputs,
    queries,
    kv_cache,
    cache_lengths,
):
    gathered = lax.all_gather(features, "tp", axis=1, tiled=True)
    gradient = lax.psum_scatter(
        lax.dot_general(
            gathered, kv_cotangent, (((0,), (0,)), ((), ())), preferred_element_type=jnp.float32
        ),
        ("learn", "dp"),
        scatter_dimension=0,
        tiled=True,
    )
    first_out = 0.9 * first_moment + 0.1 * gradient
    second_out = 0.999 * second_moment + 0.001 * gradient * gradient
    update = first_out / first_fix / (jnp.sqrt(second_out / second_fix) + 1e-08)
    master_out = master_weight - learn_rate * (update + decay_rate * master_weight)
    rollout_weight = master_out.astype(jnp.bfloat16)
    projected = jnp.einsum(
        "srk,kc->src",
        decode_inputs,
        lax.all_gather(rollout_weight, ("learn", "dp"), axis=0, tiled=True),
        preferred_element_type=jnp.float32,
    )
    new_kv = projected.astype(jnp.bfloat16)
    attended = attend(queries, kv_cache, cache_lengths, new_kv)
    return (master_out, first_out, second_out, new_kv, attended)


def solution(mesh):
    in_specs = (
        P(("learn", "dp"), "tp"),
        P(("learn", "dp"), "tp"),
        P(("learn", "dp"), "tp"),
        P(("learn", "dp"), "tp"),
        P(("learn", "dp"), "tp"),
        P(None, ("learn", "dp"), None),
        P(None, ("learn", "dp"), "tp"),
        P(None, ("learn", "dp"), "tp", None, None),
        P(("learn", "dp")),
    )
    out_specs = (
        P(("learn", "dp"), "tp"),
        P(("learn", "dp"), "tp"),
        P(("learn", "dp"), "tp"),
        P(None, ("learn", "dp"), "tp"),
        P(None, ("learn", "dp"), "tp"),
    )
    return jax.shard_map(shards, mesh=mesh, in_specs=in_specs, out_specs=out_specs, check_vma=False)
```

profile of v0, /device:TPU:18, one launch (start us, length us, event | category | flops | bytes accessed | tf_op | source)
XLA Modules:
  0.0 399.8 jit_solution(16661028505991461577)
XLA Ops:
  7.2 0.0 copy-start
  7.2 0.0 all-gather.3.cloned.1.call-start
  7.2 0.7 all-gather.3.cloned.1.call-update
  7.9 0.0 reduce-scatter.2.cloned.1.call-start
  8.0 90.0 %all-gather.3.cloned.1.call-done = bf16[512,8192]{1,0:T(8,128)(2,1)} async-done(((bf16[512,2048]{1,0:T(8,128)(2,1)}), bf16[512,8192]{1,0:T(8,128)(2,1)}) %all-gather.3.cloned.1.call-update) | async-done | bytes 8388624 | tf_op jit(solution)/shard_map/all_gather | solution.py:67
  98.0 0.0 copy-done
  98.0 11.7 %fusion.37 = f32[8192,512]{1,0:T(8,128)} fusion(bf16[512,8192]{1,0:T(8,128)(2,1)} %all-gather.3.cloned.1.call-done, bf16[512,512]{1,0:T(8,128)(2,1)S(1)} %copy-done), kind=kOutput, calls=%fused_computation.44 | convolution fusion | flops 4294967296 | bytes 25690112 | tf_op jit(solution)/shard_map/dot_general | solution.py:69
  109.7 0.0 copy-start.1
  109.7 0.0 copy-start.2
  109.7 0.0 copy-start.6
  109.7 0.0 reduce-scatter.2.cloned.1.call-update
  109.7 0.0 all-gather.5.cloned.1.call-start
  109.8 189.9 %reduce-scatter.2.cloned.1.call-done = f32[128,512]{1,0:T(8,128)} async-done(((f32[8192,512]{1,0:T(8,128)}), f32[128,512]{1,0:T(8,128)}) %reduce-scatter.2.cloned.1.call-update) | async-done | bytes 262160 | tf_op jit(solution)/shard_map/reduce_scatter | solution.py:68
  299.6 0.0 copy-done.1
  299.6 0.0 copy-done.2
  299.6 0.0 copy-done.3
  299.6 2.0 fusion.32
  301.6 0.0 all-gather.5.cloned.1.call-update
  301.7 0.0 copy-done.5
  301.7 0.0 copy-done.6
  301.7 0.1 iota_compare_fusion
  301.8 0.0 copy-start.4
  301.8 3.8 fusion.35
  305.6 77.8 %all-gather.5.cloned.1.call-done = bf16[8192,512]{1,0:T(8,128)(2,1)} async-done(((bf16[128,512]{1,0:T(8,128)(2,1)}), bf16[8192,512]{1,0:T(8,128)(2,1)}) %all-gather.5.cloned.1.call-update) | async-done | bytes 8388624 | tf_op jit(solution)/shard_map/all_gather | solution.py:84
  383.4 0.0 copy-done.4
  383.4 4.6 %fusion.20 = bf16[4,2,512]{2,0,1:T(4,128)(2,1)S(1)} fusion(bf16[8192,512]{1,0:T(8,128)(2,1)} %all-gather.5.cloned.1.call-done, bf16[4,2,8192]{2,1,0:T(2,128)(2,1)S(1)} %copy-done.4), kind=kOutput, calls=%fused_computation.21 | convolution fusion | flops 67112960 | bytes 8527872 | tf_op jit(solution)/shard_map/srk,kc->src/dot_general | solution.py:81
  387.9 0.6 copy.26
  388.6 0.3 fusion.36
  388.9 0.4 fusion.9
  389.4 3.0 fusion.10
  392.4 0.2 fusion.14
  392.6 0.6 convert_element_type.27
  (10 shorter events, 0.1 us)
Async XLA Ops:
  7.2 90.8 %copy-start = (bf16[512,512]{1,0:T(8,128)(2,1)S(1)}, bf16[512,512]{1,0:T(8,128)(2,1)}, u32[]{:S(2)}) copy-start(bf16[512,512]{1,0:T(8,128)(2,1)} %param.10) | copy-start | bytes 1572868
  7.2 90.8 %all-gather.3.cloned.1.call-start = ((), (), s32[]{:S(2)}) async-start(), calls=%async_computation.1 | async-start | bytes 10485760 | tf_op jit(solution)/shard_map/all_gather | solution.py:67
  7.9 291.7 %reduce-scatter.2.cloned.1.call-start = ((), (), s32[]{:S(2)}) async-start(), calls=%async_computation.2 | async-start | bytes 17039360 | tf_op jit(solution)/shard_map/reduce_scatter | solution.py:68
  109.7 190.0 %copy-start.1 = (f32[128,512]{1,0:T(8,128)S(1)}, f32[128,512]{1,0:T(8,128)}, u32[]{:S(2)}) copy-start(f32[128,512]{1,0:T(8,128)} %param.11) | copy-start | bytes 786436
  109.7 190.0 %copy-start.2 = (f32[128,512]{1,0:T(8,128)S(1)}, f32[128,512]{1,0:T(8,128)}, u32[]{:S(2)}) copy-start(f32[128,512]{1,0:T(8,128)} %param.12) | copy-start | bytes 786436
  109.7 190.0 %copy-start.3 = (f32[128,512]{1,0:T(8,128)S(1)}, f32[128,512]{1,0:T(8,128)}, u32[]{:S(2)}) copy-start(f32[128,512]{1,0:T(8,128)} %param.13) | copy-start | bytes 786436
  109.7 192.0 %copy-start.5 = (bf16[4,2,2048]{2,1,0:T(2,128)(2,1)S(1)}, bf16[4,2,2048]{2,1,0:T(2,128)(2,1)}, u32[]{:S(2)}) copy-start(bf16[4,2,2048]{2,1,0:T(2,128)(2,1)} %param.15) | copy-start | bytes 98308
  109.7 192.0 %copy-start.6 = (s32[2]{0:T(128)S(1)}, s32[2]{0:T(128)}, u32[]{:S(2)}) copy-start(s32[2]{0:T(128)} %param.17) | copy-start | bytes 28
  109.7 273.6 %all-gather.5.cloned.1.call-start = ((), (), s32[]{:S(2)}) async-start(), calls=%async_computation.3 | async-start | bytes 8519680 | tf_op jit(solution)/shard_map/all_gather | solution.py:84
  301.8 81.6 %copy-start.4 = (bf16[4,2,8192]{2,1,0:T(2,128)(2,1)S(1)}, bf16[4,2,8192]{2,1,0:T(2,128)(2,1)}, u32[]{:S(2)}) copy-start(bf16[4,2,8192]{2,1,0:T(2,128)(2,1)} %param.14) | copy-start | bytes 393220
Sparse Core Ops, SparseCore 0:
  9.8 88.1 all-gather.2
  109.8 189.7 reduce-scatter.1
  302.4 80.8 all-gather.4
where the time goes:
time: 403 us; the launch traced here: 400 us
  waiting for transfers between devices  358 us (89%)
  matrix products  23.5 us (6%)
  between operations  13.9 us (3%)
    reduce_scatter x1, waiting for transfers between devices, shards(): lax.psum_scatter(lax.dot_general(gathered, kv_cotangent, (((0,), (0,)), (...  190 us
    all_gather x1, waiting for transfers between devices, shards(): gathered = lax.all_gather(features, 'tp', axis=1, tiled=True)  90 us
    all_gather x1, waiting for transfers between devices, shards(): lax.all_gather(rollout_weight, ('learn', 'dp'), axis=0, tiled=True)  77.8 us
    dot_general x1, matrix products, shards(): lax.dot_general(gathered, kv_cotangent, (((0,), (0,)), ((), ())), preferr...  11.7 us
  transfers between devices with their start and end apart: 3, of which 3 were waited for; matrix products, arithmetic and copies ran while one was open for 1% of the time, Pallas kernels for 0%

commit v1 on v0

--- a/solution.py
+++ b/solution.py
@@ -64,26 +64,36 @@
     kv_cache,
     cache_lengths,
 ):
-    gathered = lax.all_gather(features, "tp", axis=1, tiled=True)
-    gradient = lax.psum_scatter(
-        lax.dot_general(
-            gathered, kv_cotangent, (((0,), (0,)), ((), ())), preferred_element_type=jnp.float32
-        ),
-        ("learn", "dp"),
-        scatter_dimension=0,
-        tiled=True,
+    token_count, own_columns = kv_cotangent.shape
+    tp_size = lax.axis_size("tp")
+    dp_size = lax.axis_size("dp")
+    learn_size = lax.axis_size("learn")
+    high = learn_size // tp_size
+    cotangents = lax.all_gather(kv_cotangent, "tp", axis=0)
+    part = own_columns // tp_size
+    cotangents = cotangents.reshape(tp_size, token_count, tp_size, part)
+    products = jnp.einsum(
+        "tr,ctsk->srck", features, cotangents, preferred_element_type=jnp.float32
     )
+    products = products.reshape(-1, tp_size * part)
+    summed = lax.psum_scatter(products, ("learn", "dp"), scatter_dimension=0, tiled=True)
+    summed = summed.reshape(-1, tp_size, part)
+    summed = lax.all_to_all(summed, "tp", 1, 0, tiled=False)
+    groups = [[one * high + low for one in range(tp_size)] for low in range(high)]
+    summed = lax.all_to_all(summed, "learn", 0, 1, axis_index_groups=groups, tiled=False)
+    gradient = summed.reshape(-1, own_columns)
     first_out = 0.9 * first_moment + 0.1 * gradient
     second_out = 0.999 * second_moment + 0.001 * gradient * gradient
     update = first_out / first_fix / (jnp.sqrt(second_out / second_fix) + 1e-08)
     master_out = master_weight - learn_rate * (update + decay_rate * master_weight)
     rollout_weight = master_out.astype(jnp.bfloat16)
-    projected = jnp.einsum(
-        "srk,kc->src",
-        decode_inputs,
-        lax.all_gather(rollout_weight, ("learn", "dp"), axis=0, tiled=True),
-        preferred_element_type=jnp.float32,
-    )
+    steps, rows, width = decode_inputs.shape
+    devices = learn_size * dp_size
+    spread = decode_inputs.reshape(steps, rows, devices, width // devices)
+    spread = lax.all_to_all(spread, ("learn", "dp"), 2, 0, tiled=False)
+    partial = jnp.einsum("nk,kc->nc", spread.reshape(-1, width // devices), rollout_weight, preferred_element_type=jnp.float32)
+    projected = lax.psum_scatter(partial, ("learn", "dp"), scatter_dimension=0, tiled=True)
+    projected = projected.reshape(steps, rows, own_columns)
     new_kv = projected.astype(jnp.bfloat16)
     attended = attend(queries, kv_cache, cache_lengths, new_kv)
     return (master_out, first_out, second_out, new_kv, attended)

time: 403 us -> 472 us (1.17)
  local copies, waits for them, and re-layouts: 1.34 us -> 43.6 us
  starting transfers between devices: 0.12 us -> 13.2 us
  waiting for transfers between devices: 358 us -> 368 us
  blocking collectives: 0 us -> 8.67 us
    all_gather x2 -> x1, waiting for transfers between devices: 168 us -> 36.8 us  [shards(): cotangents = lax.all_gather(kv_cotangent, 'tp', axis=0)]
    reduce_scatter x1 -> x2, waiting for transfers between devices: 190 us -> 318 us  [the longest x1 190 us: shards(): lax.psum_scatter(products, ('learn', 'dp'), scatter_dimension=0, tiled=True)]
    transpose x0 -> x1, local copies, waits for them, and re-layouts: none -> 19.3 us  [shards(): jnp.einsum('tr,ctsk->srck', features, cotangents, preferred_element_type=...]
    unnamed x15 -> x26, local copies, waits for them, and re-layouts: 0.65 us -> 16.9 us
    all_to_all x0 -> x2, starting transfers between devices: none -> 13.1 us  [the longest x1 8.29 us: shards(): spread = lax.all_to_all(spread, ('learn', 'dp'), 2, 0, tiled=False)]
    all_to_all x0 -> x2, waiting for transfers between devices: none -> 12.9 us  [the longest x1 9 us: shards(): spread = lax.all_to_all(spread, ('learn', 'dp'), 2, 0, tiled=False)]
    all_to_all x0 -> x1, blocking collectives: none -> 8.67 us  [shards(): summed = lax.all_to_all(summed, 'tp', 1, 0, tiled=False)]
    dot_general x2, matrix products: 16.2 us -> 10.1 us  [the longest x1 9.77 us: shards(): jnp.einsum('tr,ctsk->srck', features, cotangents, preferred_element_type=...]
  transfers between devices with their start and end apart: 3 -> 5, of which waited for: 3 -> 5; matrix products, arithmetic and copies ran while one was open for 1% -> 2% of each run, Pallas kernels for 0% -> 0%
where the time goes in v1:
time: 472 us; the launch traced here: 470 us
  waiting for transfers between devices  368 us (78%)
  local copies, waits for them, and re-layouts  43.6 us (9%)
  matrix products  18.8 us (4%)
  between operations  14 us (3%)
  starting transfers between devices  13.2 us (3%)
  blocking collectives  8.67 us (2%)
    reduce_scatter x1, waiting for transfers between devices, shards(): lax.psum_scatter(products, ('learn', 'dp'), scatter_dimension=0, tiled=True)  190 us
    reduce_scatter x1, waiting for transfers between devices, shards(): lax.psum_scatter(partial, ('learn', 'dp'), scatter_dimension=0, tiled=True)  128 us
    all_gather x1, waiting for transfers between devices, shards(): cotangents = lax.all_gather(kv_cotangent, 'tp', axis=0)  36.8 us
    transpose x1, local copies, waits for them, and re-layouts, shards(): jnp.einsum('tr,ctsk->srck', features, cotangents, preferred_element_type=...  19.3 us
    unnamed x26, local copies, waits for them, and re-layouts  16.9 us
    dot_general x1, matrix products, shards(): jnp.einsum('tr,ctsk->srck', features, cotangents, preferred_element_type=...  9.77 us
  transfers between devices with their start and end apart: 5, of which 5 were waited for; matrix products, arithmetic and copies ran while one was open for 2% of the time, Pallas kernels for 0%

profile of v1, /device:TPU:18, one launch (start us, length us, event | category | flops | bytes accessed | tf_op | source)
XLA Modules:
  0.0 469.6 jit_solution(8143155068164671595)
XLA Ops:
  7.2 0.7 all-gather.3.cloned.1.call-update
  8.0 36.8 %all-gather.3.cloned.1.call-done = bf16[2048,512]{1,0:T(8,128)(2,1)} async-done(((bf16[512,512]{1,0:T(8,128)(2,1)}), bf16[2048,512]{1,0:T(8,128)(2,1)}) %all-gather.3.cloned.1.call-update) | async-done | bytes 2097168 | tf_op jit(solution)/shard_map/all_gather | solution.py:72
  44.8 4.0 reshape.68
  48.8 9.8 %convolution_bitcast_fusion = f32[4,2048,4,128]{1,3,0,2:T(8,128)} fusion(bf16[512,2048]{1,0:T(8,128)(2,1)S(1)} %copy-done, bf16[4,512,4,128]{3,2,1,0:T(4,128)(2,1)} %reshape.68), kind=kOutput, calls=%fused_computation.1 | convolution fusion | flops 4294967296 | bytes 20971520 | tf_op jit(solution)/shard_map/tr,ctsk->srck/dot_general | solution.py:75
  58.5 19.3 %copy.62 = f32[4,2048,4,128]{3,2,1,0:T(4,128)} copy(f32[4,2048,4,128]{1,3,0,2:T(8,128)} %convolution_bitcast_fusion) | data formatting | bytes 33554432 | tf_op jit(solution)/shard_map/tr,ctsk->srck/transpose | solution.py:75
  77.8 12.7 %copy.106 = f32[1024,8,4,128]{3,1,2,0:T(8,128)} copy(f32[1024,8,4,128]{3,2,1,0:T(4,128)} %bitcast.86) | data formatting | bytes 33554432
  90.6 189.8 %reduce-scatter.5.cloned.1.call-done = f32[128,512]{1,0:T(8,128)} async-done(((f32[8192,512]{1,0:T(8,128)}), f32[128,512]{1,0:T(8,128)}) %reduce-scatter.5.cloned.1.call-update) | async-done | bytes 262160 | tf_op jit(solution)/shard_map/reduce_scatter | solution.py:79
  280.4 1.0 broadcast_in_dim_reshape.6
  281.5 8.7 %all_to_all.48 = f32[1,128,4,128]{3,1,0,2:T(8,128)} all-to-all(f32[1,128,4,128]{3,1,0,2:T(8,128)S(1)} %copy.63), channel_id=1, replica_groups=mesh['learn'=16,'tp'=4,'dp'=4] {'tp'}, dimensions={2} | all-to-all | bytes 524288 | tf_op jit(solution)/shard_map/all_to_all | solution.py:81
  290.1 4.8 %all-to-all-start.1 = ((f32[4,128,1,128]{3,1,2,0:T(8,128)}), f32[4,128,1,128]{3,1,2,0:T(8,128)S(1)}, u32[]{:S(2)}, u32[]{:S(2)}) async-start(f32[4,128,1,128]{3,1,2,0:T(8,128)} %bitcast.6), calls=%async_computation.2 | async-start | bytes 524288 | tf_op jit(solution)/shard_map/all_to_all | solution.py:83
  295.1 0.1 copy.66
  295.2 0.1 copy.68
  295.5 0.8 copy.69
  296.2 3.9 all-to-all-done.1
  300.1 8.3 %all-to-all-start.2 = ((bf16[1,4,2,64,128]{4,2,1,0,3:T(2,128)(2,1)}), bf16[1,4,2,64,128]{4,2,1,0,3:T(2,128)(2,1)S(1)}, u32[]{:S(2)}, u32[]{:S(2)}) async-start(bf16[1,4,2,64,128]{4,2,1,0,3:T(2,128)(2,1)} %copy.69), calls=%async_computation.3 | async-start | bytes 262144 | tf_op jit(solution)/shard_map/all_to_all | solution.py:93
  308.5 0.1 copy.65
  308.6 0.2 multiply_subtract_fusion
  308.8 9.0 %all-to-all-done.2 = bf16[1,4,2,64,128]{4,2,1,0,3:T(2,128)(2,1)S(1)} async-done(((bf16[1,4,2,64,128]{4,2,1,0,3:T(2,128)(2,1)}), bf16[1,4,2,64,128]{4,2,1,0,3:T(2,128)(2,1)S(1)}, u32[]{:S(2)}, u32[]{:S(2)}) %all-to-all-start.2) | async-done | bytes 131104 | tf_op jit(solution)/shard_map/all_to_all | solution.py:93
  317.8 0.3 convolution_bitcast_fusion.1
  318.1 1.3 copy.84
  319.6 5.0 %fusion.30 = (f32[4,2,2,8]{3,0,2,1:T(4,128)S(1)}, f32[4,2,2,8,4096]{4,3,0,2,1:T(8,128)}) fusion(bf16[4,2,2,8,128]{4,3,2,1,0:T(8,128)(2,1)S(1)} %reshape.70, bf16[2,2,2,4096,128]{4,3,2,1,0:T(8,128)(2,1)} %param.16, pred[2,4096]{1,0:T(4,128)(4,1)S(1)} %iota_compare_fusion), kind=kOutput, calls=%fused_computation.43 | convolution fusion | flops 135790464 | bytes 6332928 | tf_op jit(solution)/shard_map/srhgd,rhpd->srhgp/dot_general | solution.py:19
  324.6 0.8 copy.76
  325.5 0.8 copy.77
  326.3 0.8 copy.78
  327.2 128.0 %reduce-scatter.7.cloned.1.call-done = f32[8,512]{1,0:T(8,128)} async-done(((f32[512,512]{1,0:T(8,128)}), f32[8,512]{1,0:T(8,128)}) %reduce-scatter.7.cloned.1.call-update) | async-done | bytes 16400 | tf_op jit(solution)/shard_map/reduce_scatter | solution.py:95
  455.1 0.7 convert_element_type.26
  455.8 0.6 convert_element_type.27
  456.5 0.3 fusion.31
  456.8 2.2 fusion.9
  459.0 3.2 fusion.10
  462.3 0.2 fusion.14
  462.5 0.6 convert_element_type.32
  (35 shorter events, 0.7 us)
Async XLA Ops:
  7.2 41.6 %copy-start = (bf16[512,2048]{1,0:T(8,128)(2,1)S(1)}, bf16[512,2048]{1,0:T(8,128)(2,1)}, u32[]{:S(2)}) copy-start(bf16[512,2048]{1,0:T(8,128)(2,1)} %param.9) | copy-start | bytes 6291460
  7.2 37.6 %all-gather.3.cloned.1.call-start = ((), (), s32[]{:S(2)}) async-start(), calls=%async_computation.6 | async-start | bytes 2621440 | tf_op jit(solution)/shard_map/all_gather | solution.py:72
  7.9 272.5 %reduce-scatter.5.cloned.1.call-start = ((), (), s32[]{:S(2)}) async-start(), calls=%async_computation.5 | async-start | bytes 17039360 | tf_op jit(solution)/shard_map/reduce_scatter | solution.py:79
  90.5 204.4 %copy-start.3 = (f32[128,512]{1,0:T(8,128)S(1)}, f32[128,512]{1,0:T(8,128)}, u32[]{:S(2)}) copy-start(f32[128,512]{1,0:T(8,128)} %param.12) | copy-start | bytes 786436
  90.5 204.5 %copy-start.4 = (f32[128,512]{1,0:T(8,128)S(1)}, f32[128,512]{1,0:T(8,128)}, u32[]{:S(2)}) copy-start(f32[128,512]{1,0:T(8,128)} %param.13) | copy-start | bytes 786436
  90.5 204.7 %copy-start.5 = (f32[128,512]{1,0:T(8,128)S(1)}, f32[128,512]{1,0:T(8,128)}, u32[]{:S(2)}) copy-start(f32[128,512]{1,0:T(8,128)} %param.11) | copy-start | bytes 786436
  90.5 204.8 %copy-start.6 = (bf16[4,2,8192]{2,1,0:T(2,128)(2,1)S(1)}, bf16[4,2,8192]{2,1,0:T(2,128)(2,1)}, u32[]{:S(2)}) copy-start(bf16[4,2,8192]{2,1,0:T(2,128)(2,1)} %param.14) | copy-start | bytes 393220
  290.1 10.0 %all-to-all-start.1 = ((f32[4,128,1,128]{3,1,2,0:T(8,128)}), f32[4,128,1,128]{3,1,2,0:T(8,128)S(1)}, u32[]{:S(2)}, u32[]{:S(2)}) async-start(f32[4,128,1,128]{3,1,2,0:T(8,128)} %bitcast.6), calls=%async_computation.2 | async-start | bytes 524288 | tf_op jit(solution)/shard_map/all_to_all | solution.py:83
  300.1 17.7 %all-to-all-start.2 = ((bf16[1,4,2,64,128]{4,2,1,0,3:T(2,128)(2,1)}), bf16[1,4,2,64,128]{4,2,1,0,3:T(2,128)(2,1)S(1)}, u32[]{:S(2)}, u32[]{:S(2)}) async-start(bf16[1,4,2,64,128]{4,2,1,0,3:T(2,128)(2,1)} %copy.69), calls=%async_computation.3 | async-start | bytes 262144 | tf_op jit(solution)/shard_map/all_to_all | solution.py:93
  308.4 146.7 %reduce-scatter.7.cloned.1.call-start = ((), (), s32[]{:S(2)}) async-start(), calls=%async_computation.7 | async-start | bytes 1064960 | tf_op jit(solution)/shard_map/reduce_scatter | solution.py:95
  317.8 1.7 copy-start.7
  317.8 1.7 copy-start.8
  456.5 2.6 copy-start.2
  459.0 4.1 copy-start.1
Sparse Core Ops, SparseCore 0:
  9.8 34.9 all-gather.2
  90.6 189.7 reduce-scatter.4
  319.6 135.4 reduce-scatter.6

commit v2 on v0

v2 whole, which is shorter than its diff:
```python
import functools
import types

import jax
import jax.numpy as jnp
from jax import lax
from jax.experimental import pallas as pl
from jax.experimental.pallas import tpu as pltpu
from jax.sharding import PartitionSpec as P

learn_rate = 0.005
decay_rate = 0.1
first_fix = 1.0 - 0.9**10
second_fix = 1.0 - 0.999**10

MESH = pl.DeviceIdType.MESH
UNITS = 8
NX, NY, NZ = 4, 4, 8
LAGS = (1, 4, 7, 10)

bf16 = jnp.bfloat16
f32 = jnp.float32


def position():
    learn, dp = lax.axis_index("learn"), lax.axis_index("dp")
    return learn // 4, lax.axis_index("tp"), (learn % 4) * 2 + dp // 2, dp % 2


def device(x, y, z, core):
    return {"learn": x * 4 + z // 2, "tp": y, "dp": (z % 2) * 2 + core}


def send(source, target, send_sem, recv_sem, where):
    return pltpu.make_async_remote_copy(
        src_ref=source,
        dst_ref=target,
        send_sem=send_sem,
        recv_sem=recv_sem,
        device_id=where,
        device_id_type=MESH,
    )


def unit_place(unit):
    pair, odd = unit // 2, unit % 2
    middle = ((pair + 1) // 2) % 2
    return middle * (1 + 2 * odd) + 2 * (pair // 3), (1 - middle) * odd + middle * (pair // 2)


def adam(gradient, master, first, second):
    first = 0.9 * first + 0.1 * gradient
    second = 0.999 * second + 0.001 * gradient * gradient
    update = (first / first_fix) / (jnp.sqrt(second / second_fix) + 1e-08)
    return master - learn_rate * (update + decay_rate * master), first, second


def scratch(rows, columns, tokens, slots, head):
    part, half = rows // 4, columns // 2
    dma = pltpu.SemaphoreType.DMA
    return dict(
        feat=pltpu.VMEM((tokens, 16 * rows), bf16),
        turned=pltpu.VMEM((2, NZ, rows, tokens), bf16),
        cot=pltpu.VMEM((UNITS, tokens, half), bf16),
        core_send=pltpu.VMEM((UNITS, NZ, 4, part, half), bf16),
        core_recv=pltpu.VMEM((UNITS, NZ, 4, part, half), bf16),
        mine=pltpu.VMEM((NZ, 4, part, half), f32),
        keep=pltpu.VMEM((UNITS, 2, 2, 4, part, half), f32),
        x1_send=pltpu.VMEM((UNITS, 2, 2, 4, part, half), bf16),
        x1_recv=pltpu.VMEM((UNITS, 2, 2, 4, part, half), bf16),
        x2_send=pltpu.VMEM((UNITS, 2, 4, part, half), bf16),
        x2_recv=pltpu.VMEM((UNITS, 2, 4, part, half), bf16),
        z_sum=pltpu.VMEM((NZ, part, half), f32),
        z_own=pltpu.VMEM((UNITS, part, half), f32),
        z_send=pltpu.VMEM((UNITS, NZ - 1, part, half), bf16),
        z_recv=pltpu.VMEM((UNITS, NZ - 1, part, half), bf16),
        t_send=pltpu.VMEM((UNITS, part, half), f32),
        grad=pltpu.VMEM((2, 4, part, half), f32),
        kv=pltpu.VMEM((2, 2, 2, slots, head), bf16),
        state=pltpu.VMEM((3, rows, columns), f32),
        rollout=pltpu.VMEM((rows, columns), bf16),
        x_mine=pltpu.VMEM((8, 64 * rows), f32),
        x_pair=pltpu.VMEM((8, 64 * rows), f32),
        xz_send=pltpu.VMEM((NZ - 1, NX, 16, rows), bf16),
        xz_recv=pltpu.VMEM((NZ - 1, NX, 16, rows), bf16),
        xx_send=pltpu.VMEM((NX - 1, NZ, 16, rows), bf16),
        xx_recv=pltpu.VMEM((NX - 1, NZ, 16, rows), bf16),
        xx_own=pltpu.VMEM((NX, 16, rows), bf16),
        x_own=pltpu.VMEM((NZ, 16, rows), bf16),
        y_part=pltpu.VMEM((NX, NZ, 2, 8, columns), f32),
        y_core=pltpu.VMEM((NX, NZ, 8, columns), f32),
        yx_send=pltpu.VMEM((NX - 1, NZ, 8, columns), f32),
        yx_recv=pltpu.VMEM((NX - 1, NZ, 8, columns), f32),
        y_sum=pltpu.VMEM((NZ, 8, columns), f32),
        yz_recv=pltpu.VMEM((NZ - 1, 8, columns), f32),
        scores=pltpu.VMEM((32, slots), f32),
        query=pltpu.VMEM((2, 8, 8, head), f32),
        answer=pltpu.VMEM((2, 8, 8, head), f32),
        att=pltpu.VMEM((2, 64, head), f32),
        top=pltpu.VMEM((2, 64, head), f32),
        total=pltpu.VMEM((2, 64, head), f32),
        load_sem=dma((7,)),
        out_sem=dma((2, 4)),
        cot_ss=dma((6,)),
        cot_rs=dma((UNITS,)),
        core_ss=dma((UNITS,)),
        core_rs=dma((UNITS,)),
        x1_ss=dma((UNITS, 2)),
        x1_rs=dma((UNITS, 2)),
        x2_ss=dma((UNITS, 2)),
        x2_rs=dma((UNITS, 2)),
        z_ss=dma((UNITS,)),
        z_rs=dma((UNITS,)),
        t_ss=dma((UNITS,)),
        t_rs=dma((2, 4)),
        xc_sem=dma((2,)),
        xz_sem=dma((2,)),
        xx_ss=dma((3,)),
        xx_rs=dma((3,)),
        yc_ss=dma((4,)),
        yc_rs=dma((4,)),
        yx_ss=dma((3,)),
        yx_rs=dma((3,)),
        yz_sem=dma((2,)),
    )


def kernel(names, *refs):
    (lengths, q_ref, x_ref, f_hbm, c_hbm, w_hbm, m_hbm, v_hbm, kv_hbm) = refs[:9]
    (grad_out, new_out, att_out) = refs[9:12]
    r = types.SimpleNamespace(**dict(zip(names, refs[12:])))
    x, y, z, core = position()
    other = 1 - core
    flip, mirror = x + 1 - 2 * (x % 2), 3 - x
    first_partner, second_partner = (flip, mirror), (mirror, flip)
    rows, columns = r.rollout.shape
    part, half = rows // 4, columns // 2
    tokens = r.feat.shape[0]
    slots, head = r.kv.shape[3:]
    scale = head**-0.5

    loads = [
        pltpu.make_async_copy(source, target, r.load_sem.at[i])
        for i, (source, target) in enumerate(
            (
                (c_hbm.at[:, pl.ds(0, half)], r.cot.at[0]),
                (f_hbm, r.feat),
                (c_hbm.at[:, pl.ds(half, half)], r.cot.at[1]),
                (kv_hbm, r.kv),
                (w_hbm, r.state.at[0]),
                (m_hbm, r.state.at[1]),
                (v_hbm, r.state.at[2]),
            )
        )
    ]
    for load in loads[:3]:
        load.start()

    for s in range(4):
        r.x_mine[2 * s : 2 * s + 2] = x_ref[s].astype(f32)

    barrier = pltpu.get_barrier_semaphore()

    def greet(where):
        pl.semaphore_signal(barrier, inc=1, device_id=where, device_id_type=MESH)

    greet(device(x, y, z, other))
    for k in range(1, NX):
        greet(device((x + k) % NX, y, z, core))
    for k in range(1, NZ):
        greet(device(x, y, (z + k) % NZ, core))
    for k in (1, NY - 1):
        greet(device(x, (y + k) % NY, z, core))
    for k in range(4):

        @pl.when(jnp.logical_or(x != y, y != k))
        def _():
            greet(device(y, k, z, core))

        @pl.when(jnp.logical_or(x != y, x != k))
        def _():
            greet(device(k, x, z, core))

    same = (4 - (x - y + 4) % 4) // 4
    pl.semaphore_wait(barrier, 1 + (NX - 1) + (NZ - 1) + 2 + 8 - 2 * same)

    def cot_copy(index, source, target, step):
        return send(
            r.cot.at[source],
            r.cot.at[target],
            r.cot_ss.at[index],
            r.cot_rs.at[target],
            device(x, (y + step) % NY, z, core),
        )

    loads[0].wait()
    cot_copy(0, 0, 2, NY - 1).start()
    cot_copy(1, 0, 3, 1).start()
    x_swap = send(r.x_mine, r.x_pair, r.xc_sem.at[0], r.xc_sem.at[1], device(x, y, z, other))
    x_swap.start()
    loads[2].wait()
    cot_copy(2, 1, 4, NY - 1).start()
    cot_copy(3, 1, 5, 1).start()
    loads[1].wait()
    for load in loads[3:]:
        load.start()

    def turn(side):
        for row_block in range(NZ):
            columns_of = pl.ds(pl.multiple_of((row_block * 2 + side) * rows, rows), rows)
            r.turned[side, row_block] = r.feat[:, columns_of].T

    def multiply(side, unit, store):
        def step(i, carry):
            left = r.turned[side, pl.ds(2 * i, 2)].reshape(2 * rows, tokens)
            product = jnp.dot(left, r.cot[unit], preferred_element_type=f32)
            store(i, product.reshape(2, 4, part, half))
            return carry

        lax.fori_loop(0, NZ // 2, step, 0)

    def core_copy(unit):
        return send(
            r.core_send.at[unit],
            r.core_recv.at[unit],
            r.core_ss.at[unit],
            r.core_rs.at[unit],
            device(x, y, z, other),
        )

    def x1_copy(unit, side):
        return send(
            r.x1_send.at[unit, side],
            r.x1_recv.at[unit, side],
            r.x1_ss.at[unit, side],
            r.x1_rs.at[unit, side],
            device(first_partner[side], y, z, core),
        )

    def x2_copy(unit, side):
        return send(
            r.x2_send.at[unit, side],
            r.x2_recv.at[unit, side],
            r.x2_ss.at[unit, side],
            r.x2_rs.at[unit, side],
            device(second_partner[side], y, z, core),
        )

    def z_copy(unit, k):
        return send(
            r.z_send.at[unit, k - 1],
            r.z_recv.at[unit, k - 1],
            r.z_ss.at[unit],
            r.z_rs.at[unit],
            device(x, y, (z + k) % NZ, core),
        )

    def z_all(unit):
        return send(
            r.z_send.at[unit],
            r.z_recv.at[unit],
            r.z_ss.at[unit],
            r.z_rs.at[unit],
            device(x, y, (z + 1) % NZ, core),
        )

    def t_copy(unit):
        away, which = unit_place(unit)
        return send(
            r.t_send.at[unit],
            r.grad.at[which, x],
            r.t_ss.at[unit],
            r.t_rs.at[which, x],
            device(y, (y + away) % NY, z, core),
        )

    def stage0(unit):
        @pl.when(unit >= 2)
        def _():
            send(
                r.cot.at[unit],
                r.cot.at[unit],
                r.cot_ss.at[0],
                r.cot_rs.at[unit],
                device(x, (y + 1) % NY, z, core),
            ).wait_recv()

        @pl.when(unit == 3)
        def _():
            cot_copy(4, 3, 6, 1).start()

        @pl.when(unit == 4)
        def _():
            cot_copy(5, 4, 7, NY - 1).start()

        def store(i, product):
            r.core_send[unit, pl.ds(2 * i, 2)] = product.astype(bf16)

        multiply(other, unit, store)
        core_copy(unit).start()

    def stage1(unit):
        def store(i, product):
            r.mine[pl.ds(2 * i, 2)] = product

        multiply(core, unit, store)
        core_copy(unit).wait()
        for side in range(2):
            partner = first_partner[side]
            away = (partner, (3 - partner, partner + 1 - 2 * (partner % 2))[side])
            for k in range(2):
                for at in range(4):
                    row_block = side * 4 + at
                    r.x1_send[unit, side, k, at] = (
                        r.mine[row_block, away[k]]
                        + r.core_recv[unit, row_block, away[k]].astype(f32)
                    ).astype(bf16)
            x1_copy(unit, side).start()
        for side in range(2):
            near = (x, second_partner[side])
            for k in range(2):
                for at in range(4):
                    row_block = side * 4 + at
                    r.keep[unit, side, k, at] = r.mine[row_block, near[k]] + r.core_recv[
                        unit, row_block, near[k]
                    ].astype(f32)

    def stage2(unit):
        for side in range(2):
            x1_copy(unit, side).wait()
            r.x2_send[unit, side] = (
                r.keep[unit, side, 1] + r.x1_recv[unit, side, 1].astype(f32)
            ).astype(bf16)
            x2_copy(unit, side).start()
        for side in range(2):
            r.keep[unit, side, 0] += r.x1_recv[unit, side, 0].astype(f32)

    def stage3(unit):
        for side in range(2):
            x2_copy(unit, side).wait()
            for at in range(4):
                r.z_sum[side * 4 + at] = r.keep[unit, side, 0, at] + r.x2_recv[
                    unit, side, at
                ].astype(f32)
        for k in (4, 3, 5, 2, 6, 1, 7):
            r.z_send[unit, k - 1] = r.z_sum[(z + k) % NZ].astype(bf16)
            z_copy(unit, k).start()
        r.z_own[unit] = r.z_sum[z]

    def stage4(unit):
        z_all(unit).wait()
        total = r.z_own[unit]
        for k in range(NZ - 1):
            total = total + r.z_recv[unit, k].astype(f32)
        away, which = unit_place(unit)
        here = jnp.logical_and(x == y, away == 0)

        @pl.when(here)
        def _():
            r.grad[which, x] = total

        @pl.when(jnp.logical_not(here))
        def _():
            r.t_send[unit] = total
            t_copy(unit).start()

    def spread_z():
        x_swap.wait()
        for k in list(range(1, NZ)) + [0]:
            block = (z + k) % NZ
            for to in range(NX):
                at = pl.ds(pl.multiple_of((to * 16 + block * 2 + core) * rows, rows), rows)
                own, pair = r.x_mine[:, at], r.x_pair[:, at]
                low, high = jnp.where(core == 0, own, pair), jnp.where(core == 0, pair, own)
                value = jnp.concatenate([low, high], axis=0).astype(bf16)
                if k > 0:
                    r.xz_send[k - 1, to] = value
                else:
                    r.xx_own[to] = value
            if k > 0:
                send(
                    r.xz_send.at[k - 1],
                    r.xz_recv.at[k - 1],
                    r.xz_sem.at[0],
                    r.xz_sem.at[1],
                    device(x, y, block, core),
                ).start()

    def xx_copy(k):
        return send(
            r.xx_send.at[k - 1],
            r.xx_recv.at[k - 1],
            r.xx_ss.at[k - 1],
            r.xx_rs.at[k - 1],
            device((x + k) % NX, y, z, core),
        )

    def spread_x():
        send(
            r.xz_send,
            r.xz_recv,
            r.xz_sem.at[0],
            r.xz_sem.at[1],
            device(x, y, (z + 1) % NZ, core),
        ).wait()
        for k in range(NX):
            to = (x + k) % NX
            target = r.x_own if k == 0 else r.xx_send.at[k - 1]
            target[z] = r.xx_own[to]
            for j in range(1, NZ):
                target[(z + NZ - j) % NZ] = r.xz_recv[j - 1, to]
            if k > 0:
                xx_copy(k).start()

    chunk = min(1024, slots)

    def cached(pair):
        row, kv_head = pair // 2, pair % 2
        query = r.query[kv_head].reshape(4, 2, 8, head)
        query = jnp.where(row == 0, query[:, 0], query[:, 1]).reshape(32, head).astype(bf16)

        def score(i, highest):
            at = pl.ds(pl.multiple_of(i * chunk, chunk), chunk)
            value = lax.dot_general(
                query,
                r.kv[0, row, kv_head, at],
                (((1,), (1,)), ((), ())),
                preferred_element_type=f32,
            )
            places = i * chunk + lax.broadcasted_iota(jnp.int32, value.shape, 1)
            value = jnp.where(places < lengths[row], value * scale, -jnp.inf)
            r.scores[:, at] = value
            return jnp.maximum(highest, jnp.max(value, axis=1, keepdims=True))

        highest = lax.fori_loop(0, slots // chunk, score, jnp.full((32, 1), -jnp.inf, f32))

        def weigh(i, carry):
            total, result = carry
            at = pl.ds(pl.multiple_of(i * chunk, chunk), chunk)
            weight = jnp.exp(r.scores[:, at] - highest)
            total = total + jnp.sum(weight, axis=1, keepdims=True)
            result = result + jnp.dot(
                weight.astype(bf16), r.kv[1, row, kv_head, at], preferred_element_type=f32
            )
            return total, result

        total, result = lax.fori_loop(
            0, slots // chunk, weigh, (jnp.zeros((32, 1), f32), jnp.zeros((32, head), f32))
        )
        highest = jnp.broadcast_to(highest, (32, head))
        total = jnp.broadcast_to(total, (32, head))
        for s in range(4):
            at = pl.ds(pl.multiple_of(s * 16 + row * 8, 8), 8)
            one = slice(s * 8, s * 8 + 8)
            r.att[kv_head, at] = result[one]
            r.top[kv_head, at] = highest[one]
            r.total[kv_head, at] = total[one]

    turn(other)

    def during(t, lag, stage):
        @pl.when(jnp.logical_and(t >= lag, t < UNITS + lag))
        def _():
            stage(t - lag)

    def tick(t, carry):
        during(t, LAGS[3], stage4)
        during(t, LAGS[2], stage3)
        during(t, LAGS[1], stage2)
        during(t, LAGS[0], stage1)
        during(t, 0, stage0)

        @pl.when(t == 0)
        def _():
            turn(core)
            spread_z()

        @pl.when(t == 2)
        def _():
            spread_x()
            loads[3].wait()
            asked = jnp.concatenate([q_ref[s].astype(f32) for s in range(4)], axis=0)
            for h in range(2):
                for g in range(8):
                    r.query[h, :, g, :] = asked[:, (h * 8 + g) * head : (h * 8 + g + 1) * head]

        during(t, 3, lambda pair: pl.when(pair < 4)(lambda: cached(pair)))

        @pl.when(t == UNITS)
        def _():
            for k in range(1, NX):
                xx_copy(k).wait()
            for k in range(4, 7):
                loads[k].wait()
            for index in range(6):
                cot_copy(index, index % 2, 2 + index, 1).wait_send()

        return carry

    lax.fori_loop(0, UNITS + LAGS[3], tick, 0)

    stores = []
    for s in range(4):
        for which in range(2):

            @pl.when(jnp.logical_or(x != y, x != s))
            def _():
                send(
                    r.t_send.at[0],
                    r.grad.at[which, s],
                    r.t_ss.at[0],
                    r.t_rs.at[which, s],
                    device(x, (y + 1) % NY, z, core),
                ).wait_recv()

            at = (pl.ds(s * part, part), pl.ds(which * half, half))
            gradient = r.grad[which, s]
            master, _, _ = adam(
                gradient, *(r.state[i, at[0], at[1]] for i in range(3))
            )
            r.rollout[at[0], at[1]] = master.astype(bf16)
            stores.append(
                pltpu.make_async_copy(
                    r.grad.at[which, s], grad_out.at[at], r.out_sem.at[which, s]
                )
            )
            stores[-1].start()

    def yc_copy(k):
        return send(
            r.y_part.at[k, :, other],
            r.y_core.at[k],
            r.yc_ss.at[k],
            r.yc_rs.at[k],
            device(x, y, z, other),
        )

    def yx_copy(k):
        return send(
            r.yx_send.at[k - 1],
            r.yx_recv.at[k - 1],
            r.yx_ss.at[k - 1],
            r.yx_rs.at[k - 1],
            device((x + NX - k) % NX, y, z, core),
        )

    for k in (2, 1, 3, 0):
        inputs = r.x_own[...] if k == 0 else r.xx_recv[k - 1]
        product = jnp.dot(
            inputs.reshape(NZ * 16, rows), r.rollout[...], preferred_element_type=f32
        )
        r.y_part[k] = product.reshape(NZ, 2, 8, columns)
        yc_copy(k).start()
    for k in (2, 1, 3):
        yc_copy(k).wait()
        r.yx_send[k - 1] = r.y_part[k, :, core] + r.y_core[k]
        yx_copy(k).start()
    yc_copy(0).wait()
    r.y_sum[...] = r.y_part[0, :, core] + r.y_core[0]
    for unit in range(UNITS):
        away, _ = unit_place(unit)

        @pl.when(jnp.logical_or(x != y, away != 0))
        def _():
            t_copy(unit).wait_send()

    for k in (1, 3, 2):
        yx_copy(k).wait()
        r.y_sum[...] += r.yx_recv[k - 1]

    def yz_copy(k):
        return send(
            r.y_sum.at[(z + k) % NZ],
            r.yz_recv.at[k - 1],
            r.yz_sem.at[0],
            r.yz_sem.at[1],
            device(x, y, (z + k) % NZ, core),
        )

    for k in (4, 3, 5, 2, 6, 1, 7):
        yz_copy(k).start()
    for store in stores:
        store.wait()
    send(
        r.y_sum.at[pl.ds(0, NZ - 1)],
        r.yz_recv,
        r.yz_sem.at[0],
        r.yz_sem.at[1],
        device(x, y, (z + 1) % NZ, core),
    ).wait()
    fresh = r.y_sum[z]
    for k in range(NZ - 1):
        fresh = fresh + r.yz_recv[k]
    for s in range(4):
        new_out[s] = fresh[2 * s : 2 * s + 2].astype(bf16)
    fresh = fresh.astype(bf16)

    line = lax.broadcasted_iota(jnp.int32, (64, 8), 0)
    spot = lax.broadcasted_iota(jnp.int32, (64, 8), 1)
    allowed = jnp.logical_and((line // 8) % 2 == spot % 2, spot // 2 <= line // 16)
    for kv_head in range(2):
        key = fresh[:, kv_head * 2 * head : (kv_head * 2 + 1) * head]
        value = fresh[:, (kv_head * 2 + 1) * head : (kv_head * 2 + 2) * head]
        score = lax.dot_general(
            r.query[kv_head].reshape(64, head).astype(bf16), key, (((1,), (1,)), ((), ())), preferred_element_type=f32
        )
        score = jnp.where(allowed, score * scale, -jnp.inf)
        before = r.top[kv_head][:, :1]
        highest = jnp.maximum(before, jnp.max(score, axis=1, keepdims=True))
        weight = jnp.exp(score - highest)
        factor = jnp.exp(before - highest)
        total = r.total[kv_head][:, :1] * factor + jnp.sum(weight, axis=1, keepdims=True)
        result = r.att[kv_head] * factor + jnp.dot(
            weight.astype(bf16), value, preferred_element_type=f32
        )
        r.answer[kv_head] = (result / total).reshape(8, 8, head)
        for g in range(8):
            value = r.answer[kv_head, :, g, :]
            at = pl.ds((kv_head * 8 + g) * head, head)
            for s in range(4):
                att_out[s, :, at] = value[2 * s : 2 * s + 2].astype(bf16)


def shards(
    features,
    kv_cotangent,
    master_weight,
    first_moment,
    second_moment,
    decode_inputs,
    queries,
    kv_cache,
    cache_lengths,
):
    tokens = features.shape[0]
    rows, columns = master_weight.shape
    steps, own_rows, width = decode_inputs.shape
    heads, slots, head = kv_cache.shape[2:]
    shapes = scratch(rows, columns, tokens, slots, head)
    in_vmem = pl.BlockSpec(memory_space=pltpu.VMEM)
    anywhere = pl.BlockSpec(memory_space=pl.ANY)
    gradient, new_kv, attended = pl.pallas_call(
        functools.partial(kernel, tuple(shapes)),
        out_shape=(
            jax.ShapeDtypeStruct((rows, columns), f32),
            jax.ShapeDtypeStruct((steps, own_rows, columns), bf16),
            jax.ShapeDtypeStruct(queries.shape, bf16),
        ),
        in_specs=[pl.BlockSpec(memory_space=pltpu.SMEM), in_vmem, in_vmem] + [anywhere] * 6,
        out_specs=(anywhere, in_vmem, in_vmem),
        scratch_shapes=list(shapes.values()),
        compiler_params=pltpu.CompilerParams(
            collective_id=0, has_side_effects=True, vmem_limit_bytes=56 * 2**20
        ),
        name="fused_step",
    )(
        cache_lengths,
        queries,
        decode_inputs,
        features,
        kv_cotangent,
        master_weight,
        first_moment,
        second_moment,
        kv_cache,
    )
    state = adam(gradient, master_weight, first_moment, second_moment)
    return (*state, new_kv, attended)


def solution(mesh):
    in_specs = (
        P(("learn", "dp"), "tp"),
        P(("learn", "dp"), "tp"),
        P(("learn", "dp"), "tp"),
        P(("learn", "dp"), "tp"),
        P(("learn", "dp"), "tp"),
        P(None, ("learn", "dp"), None),
        P(None, ("learn", "dp"), "tp"),
        P(None, ("learn", "dp"), "tp", None, None),
        P(("learn", "dp")),
    )
    out_specs = (
        P(("learn", "dp"), "tp"),
        P(("learn", "dp"), "tp"),
        P(("learn", "dp"), "tp"),
        P(None, ("learn", "dp"), "tp"),
        P(None, ("learn", "dp"), "tp"),
    )
    return jax.shard_map(shards, mesh=mesh, in_specs=in_specs, out_specs=out_specs, check_vma=False)
```

time: 403 us -> 88.3 us (0.22)
  waiting for transfers between devices: 358 us -> 0 us
  Pallas kernels: 0 us -> 81.8 us
  matrix products: 23.5 us -> 0 us
  between operations: 13.9 us -> 0.69 us
    reduce_scatter x1 -> x0, waiting for transfers between devices: 190 us -> none  [shards(): lax.psum_scatter(lax.dot_general(gathered, kv_cotangent, (((0,), (0,)), (...]
    all_gather x2 -> x0, waiting for transfers between devices: 168 us -> none  [the longest x1 90 us: shards(): gathered = lax.all_gather(features, 'tp', axis=1, tiled=True)]
    pallas_call x0 -> x1, Pallas kernels: none -> 81.8 us  [shards(): pl.pallas_call(functools.partial(kernel, tuple(shapes)), out_shape=(jax.S...]
    dot_general x6 -> x0, matrix products: 23.5 us -> none  [the longest x1 11.7 us: shards(): lax.dot_general(gathered, kv_cotangent, (((0,), (0,)), ((), ())), preferr...]
  transfers between devices with their start and end apart: 3 -> 0, of which waited for: 3 -> 0; matrix products, arithmetic and copies ran while one was open for 1% -> 0% of each run, Pallas kernels for 0% -> 0%
where the time goes in v2:
time: 88.3 us; the launch traced here: 87.1 us
  Pallas kernels  81.8 us (93%)
  local copies, waits for them, and re-layouts  2.71 us (3%)
  other arithmetic  1.95 us (2%)
    pallas_call x1, Pallas kernels, shards(): pl.pallas_call(functools.partial(kernel, tuple(shapes)), out_shape=(jax.S...  81.8 us
    unnamed x8, local copies, waits for them, and re-layouts  2.71 us
    sub x1, other arithmetic, adam(): return (master - learn_rate * (update + decay_rate * master), first, second)  1.95 us

profile of v2, /device:TPU:18, one launch (start us, length us, event | category | flops | bytes accessed | tf_op | source)
XLA Modules:
  0.0 87.1 jit_solution(11286623949394567093)
XLA Ops:
  0.6 0.0 copy-start.2
  0.6 0.0 copy-start.1
  0.7 0.0 copy-start
  0.7 81.8 %fused_step.1 = (f32[128,512]{1,0:T(8,128)}, bf16[4,2,512]{2,1,0:T(2,128)(2,1)}, bf16[4,2,2048]{2,1,0:T(2,128)(2,1)}) custom-call(s32[2]{0:T(128)} %refs_0_.1, bf16[4,2,2048]{2,1,0:T(2,128)(2,1)} %refs_1_.1, bf16[4,2,8192]{2,1,0:T(2,128)(2,1)} %refs_2_.1, bf16[512,2048]{1,0:T(8,128)(2,1)} %refs_3_.1, bf16[512,512]{1,0:T(8,128)(2,1)} %refs_4_.1, ...), custom_call_target="tpu_custom_call" | custom-call | tf_op jit(solution)/shard_map/fused_step/pallas_call | solution.py:642
  82.5 0.0 copy-done.2
  82.5 0.0 copy-done.1
  82.5 0.0 copy-done
  82.5 2.0 %multiply_subtract_fusion = (f32[128,512]{1,0:T(8,128)}, f32[128,512]{1,0:T(8,128)}, f32[128,512]{1,0:T(8,128)}) fusion(f32[128,512]{1,0:T(8,128)S(1)} %copy-done, f32[128,512]{1,0:T(8,128)} %get-tuple-element.8, f32[128,512]{1,0:T(8,128)S(1)} %copy-done.1, f32[128,512]{1,0:T(8,128)S(1)} %copy-done.2), kind=kLoop, calls=%fused_computation.2 | loop fusion | flops 983040 | bytes 1835008 | tf_op jit(solution)/shard_map/sub | solution.py:55
  84.5 1.3 %copy.16 = bf16[4,2,512]{2,1,0:T(2,128)(2,1)} copy(bf16[4,2,512]{2,1,0:T(2,128)(2,1)} %get-tuple-element.22) | data formatting | bytes 16384
  85.8 1.4 %copy.17 = bf16[4,2,2048]{2,1,0:T(2,128)(2,1)} copy(bf16[4,2,2048]{2,1,0:T(2,128)(2,1)} %get-tuple-element.23) | data formatting | bytes 65536
Async XLA Ops:
  0.6 81.8 %copy-start.2 = (f32[128,512]{1,0:T(8,128)S(1)}, f32[128,512]{1,0:T(8,128)}, u32[]{:S(2)}) copy-start(f32[128,512]{1,0:T(8,128)} %refs_7_.1) | copy-start | bytes 786436
  0.6 81.8 %copy-start.1 = (f32[128,512]{1,0:T(8,128)S(1)}, f32[128,512]{1,0:T(8,128)}, u32[]{:S(2)}) copy-start(f32[128,512]{1,0:T(8,128)} %refs_6_.1) | copy-start | bytes 786436
  0.7 81.8 %copy-start = (f32[128,512]{1,0:T(8,128)S(1)}, f32[128,512]{1,0:T(8,128)}, u32[]{:S(2)}) copy-start(f32[128,512]{1,0:T(8,128)} %refs_5_.1) | copy-start | bytes 786436

commit v3 on v2

v3 whole, which is shorter than its diff:
```python
import functools
import types

import jax
import jax.numpy as jnp
from jax import lax
from jax.experimental import pallas as pl
from jax.experimental.pallas import tpu as pltpu
from jax.sharding import PartitionSpec as P

learn_rate = 0.005
decay_rate = 0.1
first_fix = 1.0 - 0.9**10
second_fix = 1.0 - 0.999**10

MESH = pl.DeviceIdType.MESH
UNITS = 8
NX, NY, NZ = 4, 4, 8
NEW = 'P'
PLACES = ((0, 0), (0, 1), (1, 0), (3, 0), (2, 0), (1, 1), (3, 1), (2, 1))
Z_UNITS = (1, 3, 6, 7)
ORDER = (
    "B0", "B1", "X0", "C0", "D0", "C1", "D1", "Y0", "A0", "F0", "B2", "E0",
    "I1", "B3", "C2", "A1", "G0", "F1", "D2", "B5", "J1", "B6", "C3", "D3",
    "C5", "D5", "C6", "E2", "H0", "K1", "D6", "B4", "B7", "I3", "C4", "E5",
    "A2", "G2", "L1", "D4", "C7", "J3", "I6", "D7", "A3", "G5", "H2", "E4",
    "K3", "I7", "J6", "G4", "H5", "J7", "K6", "L3", "K7", "H4", "L6", "P0",
    "L7", "Q0", "P1", "Q1", "R0", "R1", "S0", "S1",
)

bf16 = jnp.bfloat16
f32 = jnp.float32


def position():
    learn, dp = lax.axis_index("learn"), lax.axis_index("dp")
    return learn // 4, lax.axis_index("tp"), (learn % 4) * 2 + dp // 2, dp % 2


def device(x, y, z, core):
    return {"learn": x * 4 + z // 2, "tp": y, "dp": (z % 2) * 2 + core}


def send(source, target, send_sem, recv_sem, where):
    return pltpu.make_async_remote_copy(
        src_ref=source,
        dst_ref=target,
        send_sem=send_sem,
        recv_sem=recv_sem,
        device_id=where,
        device_id_type=MESH,
    )


def adam(gradient, master, first, second):
    first = 0.9 * first + 0.1 * gradient
    second = 0.999 * second + 0.001 * gradient * gradient
    update = (first / first_fix) / (jnp.sqrt(second / second_fix) + 1e-08)
    return master - learn_rate * (update + decay_rate * master), first, second


def scratch(rows, columns, tokens, slots, head):
    part, half = rows // 4, columns // 2
    dma = pltpu.SemaphoreType.DMA
    return dict(
        feat=pltpu.VMEM((tokens, 16 * rows), bf16),
        turned=pltpu.VMEM((2, NZ, rows, tokens), bf16),
        cot=pltpu.VMEM((UNITS, tokens, half), bf16),
        core_send=pltpu.VMEM((UNITS, NZ, 4, part, half), bf16),
        core_recv=pltpu.VMEM((UNITS, NZ, 4, part, half), bf16),
        mine=pltpu.VMEM((NZ, 4, part, half), f32),
        keep=pltpu.VMEM((UNITS, 2, 2, 4, part, half), f32),
        x1_send=pltpu.VMEM((UNITS, 2, 2, 4, part, half), bf16),
        x1_recv=pltpu.VMEM((UNITS, 2, 2, 4, part, half), bf16),
        x2_send=pltpu.VMEM((UNITS, 2, 4, part, half), bf16),
        x2_recv=pltpu.VMEM((UNITS, 2, 4, part, half), bf16),
        a_send=pltpu.VMEM((len(Z_UNITS), 2, 2, 4, part, half), bf16),
        a_recv=pltpu.VMEM((len(Z_UNITS), 2, 2, 4, part, half), bf16),
        a_keep=pltpu.VMEM((len(Z_UNITS), 2, 2, 4, part, half), f32),
        b_keep=pltpu.VMEM((len(Z_UNITS), 2, 2, 2, part, half), f32),
        b_send=pltpu.VMEM((len(Z_UNITS), 2, 2, 2, part, half), bf16),
        b_recv=pltpu.VMEM((len(Z_UNITS), 2, 2, 2, part, half), bf16),
        c_send=pltpu.VMEM((len(Z_UNITS), 2, 2, part, half), bf16),
        c_recv=pltpu.VMEM((len(Z_UNITS), 2, 2, part, half), bf16),
        d_sum=pltpu.VMEM((4, part, half), f32),
        d_send=pltpu.VMEM((len(Z_UNITS), 3, part, half), bf16),
        d_recv=pltpu.VMEM((len(Z_UNITS), 3, part, half), bf16),
        a_ss=dma((len(Z_UNITS), 2)),
        a_rs=dma((len(Z_UNITS), 2)),
        b_ss=dma((len(Z_UNITS), 2)),
        b_rs=dma((len(Z_UNITS), 2)),
        c_ss=dma((len(Z_UNITS), 2)),
        c_rs=dma((len(Z_UNITS), 2)),
        d_ss=dma((len(Z_UNITS),)),
        d_rs=dma((len(Z_UNITS),)),
        z_sum=pltpu.VMEM((NZ, part, half), f32),
        z_own=pltpu.VMEM((UNITS, part, half), f32),
        z_send=pltpu.VMEM((UNITS, NZ - 1, part, half), bf16),
        z_recv=pltpu.VMEM((UNITS, NZ - 1, part, half), bf16),
        t_send=pltpu.VMEM((UNITS, part, half), f32),
        grad=pltpu.VMEM((2, 4, part, half), f32),
        kv=pltpu.VMEM((2, 2, 2, slots, head), bf16),
        state=pltpu.VMEM((3, rows, columns), f32),
        rollout=pltpu.VMEM((rows, columns), bf16),
        x_mine=pltpu.VMEM((2, 32, 8, rows), f32),
        x_pair=pltpu.VMEM((32, 8, rows), f32),
        xz_send=pltpu.VMEM((NZ - 1, NX, 16, rows), bf16),
        xz_recv=pltpu.VMEM((NZ - 1, NX, 16, rows), bf16),
        xx_send=pltpu.VMEM((NX - 1, NZ, 16, rows), bf16),
        xx_recv=pltpu.VMEM((NX - 1, NZ, 16, rows), bf16),
        xx_own=pltpu.VMEM((NZ, 16, rows), bf16),
        x_all=pltpu.VMEM((NX, NZ, 16, rows), bf16),
        y_part=pltpu.VMEM((2, NX, NZ, 2, 8, half), f32),
        y_core=pltpu.VMEM((2, NX, NZ, 8, half), f32),
        yx_send=pltpu.VMEM((2, NX - 1, NZ, 8, half), f32),
        yx_recv=pltpu.VMEM((2, NX - 1, NZ, 8, half), f32),
        y_sum=pltpu.VMEM((2, NZ, 8, half), f32),
        yz_recv=pltpu.VMEM((2, NZ - 1, 8, half), f32),
        scores=pltpu.VMEM((32, slots), f32),
        query=pltpu.VMEM((2, 8, 8, head), f32),
        answer=pltpu.VMEM((2, 8, 8, head), f32),
        att=pltpu.VMEM((2, 64, head), f32),
        top=pltpu.VMEM((2, 64, head), f32),
        total=pltpu.VMEM((2, 64, head), f32),
        load_sem=dma((7,)),
        out_sem=dma((2, 4)),
        cot_ss=dma((6,)),
        cot_rs=dma((UNITS,)),
        core_ss=dma((UNITS,)),
        core_rs=dma((UNITS,)),
        x1_ss=dma((UNITS, 2)),
        x1_rs=dma((UNITS, 2)),
        x2_ss=dma((UNITS, 2)),
        x2_rs=dma((UNITS, 2)),
        z_ss=dma((UNITS,)),
        z_rs=dma((UNITS,)),
        t_ss=dma((UNITS,)),
        t_rs=dma((2, 4)),
        xc_sem=dma((2,)),
        xz_sem=dma((2,)),
        xx_ss=dma((3,)),
        xx_rs=dma((3,)),
        yc_ss=dma((2, 4)),
        yc_rs=dma((2, 4)),
        yx_ss=dma((2, 3)),
        yx_rs=dma((2, 3)),
        yz_sem=dma((2, 2)),
    )


def kernel(names, *refs):
    (lengths, q_ref, x_ref, f_hbm, c_hbm, w_hbm, m_hbm, v_hbm, kv_hbm) = refs[:9]
    (grad_out, new_out, att_out) = refs[9:12]
    r = types.SimpleNamespace(**dict(zip(names, refs[12:])))
    x, y, z, core = position()
    other = 1 - core
    flip, mirror = x + 1 - 2 * (x % 2), 3 - x
    first_partner, second_partner = (flip, mirror), (mirror, flip)
    rows, columns = r.rollout.shape
    part, half = rows // 4, columns // 2
    tokens = r.feat.shape[0]
    slots, head = r.kv.shape[3:]
    scale = head**-0.5

    loads = [
        pltpu.make_async_copy(source, target, r.load_sem.at[i])
        for i, (source, target) in enumerate(
            (
                (c_hbm.at[:, pl.ds(0, half)], r.cot.at[0]),
                (f_hbm, r.feat),
                (c_hbm.at[:, pl.ds(half, half)], r.cot.at[1]),
                (kv_hbm, r.kv),
                (w_hbm, r.state.at[0]),
                (m_hbm, r.state.at[1]),
                (v_hbm, r.state.at[2]),
            )
        )
    ]
    for load in loads[:3]:
        load.start()

    inputs = jnp.concatenate([x_ref[s].astype(f32) for s in range(4)], axis=0)
    for block in range(64):
        r.x_mine[block % 2, block // 2] = inputs[:, block * rows : (block + 1) * rows]

    barrier = pltpu.get_barrier_semaphore()

    def greet(where):
        pl.semaphore_signal(barrier, inc=1, device_id=where, device_id_type=MESH)

    greet(device(x, y, z, other))
    for k in range(1, NX):
        greet(device((x + k) % NX, y, z, core))
    for k in range(1, NZ):
        greet(device(x, y, (z + k) % NZ, core))
    for k in range(1, NY):
        greet(device(x, (y + k) % NY, z, core))
    for k in range(4):

        @pl.when(jnp.logical_or(x != y, y != k))
        def _():
            greet(device(y, k, z, core))

        @pl.when(jnp.logical_or(x != y, x != k))
        def _():
            greet(device(k, x, z, core))

    same = (4 - (x - y + 4) % 4) // 4
    pl.semaphore_wait(barrier, 1 + (NX - 1) + (NZ - 1) + (NY - 1) + 8 - 2 * same)

    slot = {place: unit for unit, place in enumerate(PLACES)}
    arrived = {slot[0, 0], slot[0, 1]}

    def cot_copy(index):
        step = (3, 1, 3, 1, 1, 3)[index]
        half_of = (0, 0, 1, 1, 0, 1)[index]
        source = slot[0, half_of] if index < 4 else slot[(3, 1)[half_of], half_of]
        target = slot[4 - step, half_of] if index < 4 else slot[2, half_of]
        return send(
            r.cot.at[source],
            r.cot.at[target],
            r.cot_ss.at[index],
            r.cot_rs.at[target],
            device(x, (y + step) % NY, z, core),
        )

    def have(unit):
        if unit not in arrived:
            arrived.add(unit)
            send(
                r.cot.at[unit],
                r.cot.at[unit],
                r.cot_ss.at[0],
                r.cot_rs.at[unit],
                device(x, (y + 1) % NY, z, core),
            ).wait_recv()

    def forward(part_of):
        have(slot[(3, 1)[part_of], part_of])
        cot_copy(4 + part_of).start()

    x_swap = send(
        r.x_mine.at[other],
        r.x_pair,
        r.xc_sem.at[0],
        r.xc_sem.at[1],
        device(x, y, z, other),
    )
    x_swap.start()
    loads[0].wait()
    for index in range(2):
        cot_copy(index).start()
    loads[2].wait()
    for index in range(2, 4):
        cot_copy(index).start()
    loads[1].wait()
    for load in loads[3:]:
        load.start()

    def turn(side):
        for row_block in range(NZ):
            columns_of = pl.ds(pl.multiple_of((row_block * 2 + side) * rows, rows), rows)
            r.turned[side, row_block] = r.feat[:, columns_of].T

    def multiply(side, unit, store):
        def step(i, carry):
            left = r.turned[side, pl.ds(2 * i, 2)].reshape(2 * rows, tokens)
            product = jnp.dot(left, r.cot[unit], preferred_element_type=f32)
            store(i, product.reshape(2, 4, part, half))
            return carry

        lax.fori_loop(0, NZ // 2, step, 0)

    def core_copy(unit):
        return send(
            r.core_send.at[unit],
            r.core_recv.at[unit],
            r.core_ss.at[unit],
            r.core_rs.at[unit],
            device(x, y, z, other),
        )

    def x1_copy(unit, side):
        return send(
            r.x1_send.at[unit, side],
            r.x1_recv.at[unit, side],
            r.x1_ss.at[unit, side],
            r.x1_rs.at[unit, side],
            device(first_partner[side], y, z, core),
        )

    def x2_copy(unit, side):
        return send(
            r.x2_send.at[unit, side],
            r.x2_recv.at[unit, side],
            r.x2_ss.at[unit, side],
            r.x2_rs.at[unit, side],
            device(second_partner[side], y, z, core),
        )

    def z_copy(unit, k):
        return send(
            r.z_send.at[unit, k - 1],
            r.z_recv.at[unit, k - 1],
            r.z_ss.at[unit],
            r.z_rs.at[unit],
            device(x, y, (z + k) % NZ, core),
        )

    def z_all(unit):
        return send(
            r.z_send.at[unit],
            r.z_recv.at[unit],
            r.z_ss.at[unit],
            r.z_rs.at[unit],
            device(x, y, (z + 1) % NZ, core),
        )

    def t_copy(unit):
        away, which = PLACES[unit]
        return send(
            r.t_send.at[unit],
            r.grad.at[which, x],
            r.t_ss.at[unit],
            r.t_rs.at[which, x],
            device(y, (y + away) % NY, z, core),
        )

    def stage0(unit):
        have(unit)

        def store(i, product):
            r.core_send[unit, pl.ds(2 * i, 2)] = product.astype(bf16)

        multiply(other, unit, store)
        core_copy(unit).start()

    def own(unit):
        if unit == 0:
            turn(core)

        def store(i, product):
            r.mine[pl.ds(2 * i, 2)] = product

        multiply(core, unit, store)

    def stage1(unit):
        core_copy(unit).wait()
        if unit in Z_UNITS:
            at_unit = Z_UNITS.index(unit)
            for side in range(2):
                for at in range(2):
                    block = 2 * (2 * side + at) + 1 - z % 2
                    r.a_send[at_unit, side, at] = (
                        r.mine[block] + r.core_recv[unit, block].astype(f32)
                    ).astype(bf16)
                a_copy(unit, side).start()
            for side in range(2):
                for at in range(2):
                    block = 2 * (2 * side + at) + z % 2
                    r.a_keep[at_unit, side, at] = r.mine[block] + r.core_recv[
                        unit, block
                    ].astype(f32)

        else:
            for side in range(2):
                partner = first_partner[side]
                away = (partner, (3 - partner, partner + 1 - 2 * (partner % 2))[side])
                for k in range(2):
                    for at in range(4):
                        row_block = side * 4 + at
                        r.x1_send[unit, side, k, at] = (
                            r.mine[row_block, away[k]]
                            + r.core_recv[unit, row_block, away[k]].astype(f32)
                        ).astype(bf16)
                x1_copy(unit, side).start()
            for side in range(2):
                near = (x, second_partner[side])
                for k in range(2):
                    for at in range(4):
                        row_block = side * 4 + at
                        r.keep[unit, side, k, at] = r.mine[row_block, near[k]] + r.core_recv[
                            unit, row_block, near[k]
                        ].astype(f32)

    def a_copy(unit, side):
        return send(
            r.a_send.at[Z_UNITS.index(unit), side],
            r.a_recv.at[Z_UNITS.index(unit), side],
            r.a_ss.at[Z_UNITS.index(unit), side],
            r.a_rs.at[Z_UNITS.index(unit), side],
            device(x, y, (z + 1 - 2 * (z % 2), (z + 7 + 2 * (z % 2)) % NZ)[side], core),
        )

    def b_copy(unit, side):
        return send(
            r.b_send.at[Z_UNITS.index(unit), side],
            r.b_recv.at[Z_UNITS.index(unit), side],
            r.b_ss.at[Z_UNITS.index(unit), side],
            r.b_rs.at[Z_UNITS.index(unit), side],
            device(first_partner[side], y, z, core),
        )

    def c_copy(unit, side):
        return send(
            r.c_send.at[Z_UNITS.index(unit), side],
            r.c_recv.at[Z_UNITS.index(unit), side],
            r.c_ss.at[Z_UNITS.index(unit), side],
            r.c_rs.at[Z_UNITS.index(unit), side],
            device(second_partner[side], y, z, core),
        )

    def d_copy(unit, k):
        return send(
            r.d_send.at[Z_UNITS.index(unit), k - 1],
            r.d_recv.at[Z_UNITS.index(unit), k - 1],
            r.d_ss.at[Z_UNITS.index(unit)],
            r.d_rs.at[Z_UNITS.index(unit)],
            device(x, y, (z + 2 * k) % NZ, core),
        )

    def d_all(unit):
        return send(
            r.d_send.at[Z_UNITS.index(unit)],
            r.d_recv.at[Z_UNITS.index(unit)],
            r.d_ss.at[Z_UNITS.index(unit)],
            r.d_rs.at[Z_UNITS.index(unit)],
            device(x, y, (z + 2) % NZ, core),
        )

    def away_and_near(side):
        partner = first_partner[side]
        away = (partner, (3 - partner, partner + 1 - 2 * (partner % 2))[side])
        return away, (x, second_partner[side])

    def z_stage2(unit):
        at_unit = Z_UNITS.index(unit)
        for side in range(2):
            a_copy(unit, side).wait()
            away, near = away_and_near(side)
            for k in range(2):
                for at in range(2):
                    r.b_send[at_unit, side, k, at] = (
                        r.a_keep[at_unit, side, at, away[k]]
                        + r.a_recv[at_unit, side, at, away[k]].astype(f32)
                    ).astype(bf16)
            b_copy(unit, side).start()
            for k in range(2):
                for at in range(2):
                    r.b_keep[at_unit, side, k, at] = r.a_keep[
                        at_unit, side, at, near[k]
                    ] + r.a_recv[at_unit, side, at, near[k]].astype(f32)

    def z_stage3(unit):
        at_unit = Z_UNITS.index(unit)
        for side in range(2):
            b_copy(unit, side).wait()
            r.c_send[at_unit, side] = (
                r.b_keep[at_unit, side, 1] + r.b_recv[at_unit, side, 1].astype(f32)
            ).astype(bf16)
            c_copy(unit, side).start()
            r.b_keep[at_unit, side, 0] += r.b_recv[at_unit, side, 0].astype(f32)

    def z_stage4(unit):
        at_unit = Z_UNITS.index(unit)
        for side in range(2):
            c_copy(unit, side).wait()
            for at in range(2):
                r.d_sum[side * 2 + at] = r.b_keep[at_unit, side, 0, at] + r.c_recv[
                    at_unit, side, at
                ].astype(f32)
        for k in (2, 1, 3):
            r.d_send[at_unit, k - 1] = r.d_sum[(z // 2 + k) % 4].astype(bf16)
            d_copy(unit, k).start()
        r.z_own[unit] = r.d_sum[z // 2]

    def z_stage5(unit):
        d_all(unit).wait()
        total = r.z_own[unit]
        for k in range(3):
            total = total + r.d_recv[Z_UNITS.index(unit), k].astype(f32)
        finish(unit, total)

    def stage2(unit):
        for side in range(2):
            x1_copy(unit, side).wait()
            r.x2_send[unit, side] = (
                r.keep[unit, side, 1] + r.x1_recv[unit, side, 1].astype(f32)
            ).astype(bf16)
            x2_copy(unit, side).start()
        for side in range(2):
            r.keep[unit, side, 0] += r.x1_recv[unit, side, 0].astype(f32)

    def stage3(unit):
        for side in range(2):
            x2_copy(unit, side).wait()
            for at in range(4):
                r.z_sum[side * 4 + at] = r.keep[unit, side, 0, at] + r.x2_recv[
                    unit, side, at
                ].astype(f32)
        for k in (4, 3, 5, 2, 6, 1, 7):
            r.z_send[unit, k - 1] = r.z_sum[(z + k) % NZ].astype(bf16)
            z_copy(unit, k).start()
        r.z_own[unit] = r.z_sum[z]

    def stage4(unit):
        z_all(unit).wait()
        total = r.z_own[unit]
        for k in range(NZ - 1):
            total = total + r.z_recv[unit, k].astype(f32)
        finish(unit, total)

    def finish(unit, total):
        away, which = PLACES[unit]

        def go():
            r.t_send[unit] = total
            t_copy(unit).start()

        if away == 0:

            @pl.when(x == y)
            def _():
                r.grad[which, x] = total

            pl.when(x != y)(go)
        else:
            go()

    def xx_copy(k):
        return send(
            r.xx_send.at[k - 1],
            r.xx_recv.at[k - 1],
            r.xx_ss.at[k - 1],
            r.xx_rs.at[k - 1],
            device((x + k) % NX, y, z, core),
        )

    def xz_copy(k, source, target):
        return send(
            source,
            target,
            r.xz_sem.at[0],
            r.xz_sem.at[1],
            device(x, y, (z + k) % NZ, core),
        )

    def spread_x(_):
        x_swap.wait()
        for k in (2, 1, 3, 0):
            target = r.xx_own if k == 0 else r.xx_send.at[k - 1]
            for block in range(NZ):
                at = (x + k) % NX * NZ + block
                mine, pair = r.x_mine[core, at], r.x_pair[at]
                low, high = jnp.where(core == 0, mine, pair), jnp.where(core == 0, pair, mine)
                target[block] = jnp.concatenate([low, high], axis=0).astype(bf16)
            if k > 0:
                xx_copy(k).start()

    def spread_z(_):
        for k in range(1, NX):
            xx_copy(k).wait()
        for k in (4, 3, 5, 2, 6, 1, 7):
            to = (z + k) % NZ
            r.xz_send[k - 1, 0] = r.xx_own[to]
            for j in range(1, NX):
                r.xz_send[k - 1, j] = r.xx_recv[j - 1, to]
            xz_copy(k, r.xz_send.at[k - 1], r.xz_recv.at[k - 1]).start()

    def spread_done():
        xz_copy(1, r.xz_send, r.xz_recv).wait()
        r.x_all[0, z] = r.xx_own[z]
        for j in range(1, NX):
            r.x_all[j, z] = r.xx_recv[j - 1, z]
        for k in range(1, NZ):
            for j in range(NX):
                r.x_all[j, (z + NZ - k) % NZ] = r.xz_recv[k - 1, j]
        for k in range(4, 7):
            loads[k].wait()

    chunk = min(1024, slots)

    def cached(pair):
        row, kv_head = pair // 2, pair % 2
        if pair == 0:
            loads[3].wait()
            asked = jnp.concatenate([q_ref[s].astype(f32) for s in range(4)], axis=0)
            for h in range(2):
                for g in range(8):
                    r.query[h, :, g, :] = asked[:, (h * 8 + g) * head : (h * 8 + g + 1) * head]
        query = r.query[kv_head].reshape(4, 2, 8, head)
        query = query[:, row].reshape(32, head).astype(bf16)

        def score(i, highest):
            at = pl.ds(pl.multiple_of(i * chunk, chunk), chunk)
            value = lax.dot_general(
                query,
                r.kv[0, row, kv_head, at],
                (((1,), (1,)), ((), ())),
                preferred_element_type=f32,
            )
            places = i * chunk + lax.broadcasted_iota(jnp.int32, value.shape, 1)
            value = jnp.where(places < lengths[row], value * scale, -jnp.inf)
            r.scores[:, at] = value
            return jnp.maximum(highest, jnp.max(value, axis=1, keepdims=True))

        highest = lax.fori_loop(0, slots // chunk, score, jnp.full((32, 1), -jnp.inf, f32))

        def weigh(i, carry):
            total, result = carry
            at = pl.ds(pl.multiple_of(i * chunk, chunk), chunk)
            weight = jnp.exp(r.scores[:, at] - highest)
            total = total + jnp.sum(weight, axis=1, keepdims=True)
            result = result + jnp.dot(
                weight.astype(bf16), r.kv[1, row, kv_head, at], preferred_element_type=f32
            )
            return total, result

        total, result = lax.fori_loop(
            0, slots // chunk, weigh, (jnp.zeros((32, 1), f32), jnp.zeros((32, head), f32))
        )
        highest = jnp.broadcast_to(highest, (32, head))
        total = jnp.broadcast_to(total, (32, head))
        for s in range(4):
            at = pl.ds(s * 16 + row * 8, 8)
            one = slice(s * 8, s * 8 + 8)
            r.att[kv_head, at] = result[one]
            r.top[kv_head, at] = highest[one]
            r.total[kv_head, at] = total[one]

    def store_copy(which, s):
        return pltpu.make_async_copy(
            r.grad.at[which, s],
            grad_out.at[pl.ds(s * part, part), pl.ds(which * half, half)],
            r.out_sem.at[which, s],
        )

    def yc_copy(which, k):
        return send(
            r.y_part.at[which, k, :, other],
            r.y_core.at[which, k],
            r.yc_ss.at[which, k],
            r.yc_rs.at[which, k],
            device(x, y, z, other),
        )

    def yx_copy(which, k):
        return send(
            r.yx_send.at[which, k - 1],
            r.yx_recv.at[which, k - 1],
            r.yx_ss.at[which, k - 1],
            r.yx_rs.at[which, k - 1],
            device((x + NX - k) % NX, y, z, core),
        )

    def yz_copy(which, k):
        return send(
            r.y_sum.at[which, (z + k) % NZ],
            r.yz_recv.at[which, k - 1],
            r.yz_sem.at[which, 0],
            r.yz_sem.at[which, 1],
            device(x, y, (z + k) % NZ, core),
        )

    def new0(which):
        if which == first_head:
            spread_done()
        for s in range(4):

            @pl.when(jnp.logical_or(x != y, x != s))
            def _():
                send(
                    r.t_send.at[0],
                    r.grad.at[which, s],
                    r.t_ss.at[0],
                    r.t_rs.at[which, s],
                    device(x, (y + 1) % NY, z, core),
                ).wait_recv()

            at = (pl.ds(s * part, part), pl.ds(which * half, half))
            master, _, _ = adam(r.grad[which, s], *(r.state[i, at[0], at[1]] for i in range(3)))
            r.rollout[at[0], at[1]] = master.astype(bf16)
        for k in (2, 1, 3, 0):
            product = jnp.dot(
                r.x_all[k].reshape(NZ * 16, rows),
                r.rollout[:, which * half : (which + 1) * half],
                preferred_element_type=f32,
            )
            r.y_part[which, k] = product.reshape(NZ, 2, 8, half)
            yc_copy(which, k).start()
        for s in range(4):
            store_copy(which, s).start()

    def new1(which):
        for k in (2, 1, 3):
            yc_copy(which, k).wait()
            r.yx_send[which, k - 1] = r.y_part[which, k, :, core] + r.y_core[which, k]
            yx_copy(which, k).start()
        yc_copy(which, 0).wait()
        r.y_sum[which] = r.y_part[which, 0, :, core] + r.y_core[which, 0]

    def new2(which):
        for k in (1, 3, 2):
            yx_copy(which, k).wait()
            r.y_sum[which] += r.yx_recv[which, k - 1]
        for k in (4, 3, 5, 2, 6, 1, 7):
            yz_copy(which, k).start()

    def new3(which):
        send(
            r.y_sum.at[which, pl.ds(0, NZ - 1)],
            r.yz_recv.at[which],
            r.yz_sem.at[which, 0],
            r.yz_sem.at[which, 1],
            device(x, y, (z + 1) % NZ, core),
        ).wait()
        fresh = r.y_sum[which, z]
        for k in range(NZ - 1):
            fresh = fresh + r.yz_recv[which, k]
        for s in range(4):
            new_out[s, :, pl.ds(which * half, half)] = fresh[2 * s : 2 * s + 2].astype(bf16)
        fresh = fresh.astype(bf16)
        key, value = fresh[:, :head], fresh[:, head:]
        line = lax.broadcasted_iota(jnp.int32, (64, 8), 0)
        spot = lax.broadcasted_iota(jnp.int32, (64, 8), 1)
        allowed = jnp.logical_and((line // 8) % 2 == spot % 2, spot // 2 <= line // 16)
        score = lax.dot_general(
            r.query[which].reshape(64, head).astype(bf16),
            key,
            (((1,), (1,)), ((), ())),
            preferred_element_type=f32,
        )
        score = jnp.where(allowed, score * scale, -jnp.inf)
        before = r.top[which][:, :1]
        highest = jnp.maximum(before, jnp.max(score, axis=1, keepdims=True))
        weight = jnp.exp(score - highest)
        factor = jnp.exp(before - highest)
        total = r.total[which][:, :1] * factor + jnp.sum(weight, axis=1, keepdims=True)
        result = r.att[which] * factor + jnp.dot(
            weight.astype(bf16), value, preferred_element_type=f32
        )
        r.answer[which] = (result / total).reshape(8, 8, head)
        for g in range(8):
            value = r.answer[which, :, g, :]
            at = pl.ds((which * 8 + g) * head, head)
            for s in range(4):
                att_out[s, :, at] = value[2 * s : 2 * s + 2].astype(bf16)

    steps = dict(
        F=forward,
        X=spread_x,
        Y=spread_z,
        A=cached,
        B=stage0,
        C=own,
        D=stage1,
        E=stage2,
        G=stage3,
        H=stage4,
        I=z_stage2,
        J=z_stage3,
        K=z_stage4,
        L=z_stage5,
        P=new0,
        Q=new1,
        R=new2,
        S=new3,
    )
    order = [(word[0], int(word[1])) for word in ORDER]
    first_head = [place for name, place in order if name == NEW][0]
    turn(other)
    for name, place in order:
        steps[name](place)
    for unit in range(UNITS):
        if PLACES[unit][0] == 0:
            pl.when(x != y)(lambda: t_copy(unit).wait_send())
        else:
            t_copy(unit).wait_send()
    for index in range(6):
        cot_copy(index).wait_send()
    for which in range(2):
        for s in range(4):
            store_copy(which, s).wait()


def last(gradient, master, first, second, new_kv, attended, *results):
    values = (*adam(gradient[...], master[...], first[...], second[...]), new_kv[...], attended[...])
    for result, value in zip(results, values):
        result[...] = value


def shards(
    features,
    kv_cotangent,
    master_weight,
    first_moment,
    second_moment,
    decode_inputs,
    queries,
    kv_cache,
    cache_lengths,
):
    tokens = features.shape[0]
    rows, columns = master_weight.shape
    steps, own_rows, width = decode_inputs.shape
    heads, slots, head = kv_cache.shape[2:]
    shapes = scratch(rows, columns, tokens, slots, head)
    in_vmem = pl.BlockSpec(memory_space=pltpu.VMEM)
    anywhere = pl.BlockSpec(memory_space=pl.ANY)
    gradient, new_kv, attended = pl.pallas_call(
        functools.partial(kernel, tuple(shapes)),
        out_shape=(
            jax.ShapeDtypeStruct((rows, columns), f32),
            jax.ShapeDtypeStruct((steps, own_rows, columns), bf16),
            jax.ShapeDtypeStruct(queries.shape, bf16),
        ),
        in_specs=[pl.BlockSpec(memory_space=pltpu.SMEM), in_vmem, in_vmem] + [anywhere] * 6,
        out_specs=(anywhere, in_vmem, in_vmem),
        scratch_shapes=list(shapes.values()),
        compiler_params=pltpu.CompilerParams(
            collective_id=0, has_side_effects=True, vmem_limit_bytes=56 * 2**20
        ),
        name="fused_step",
    )(
        cache_lengths,
        queries,
        decode_inputs,
        features,
        kv_cotangent,
        master_weight,
        first_moment,
        second_moment,
        kv_cache,
    )
    like = jax.ShapeDtypeStruct((rows, columns), f32)
    return pl.pallas_call(
        last,
        out_shape=(
            like,
            like,
            like,
            jax.ShapeDtypeStruct(new_kv.shape, bf16),
            jax.ShapeDtypeStruct(attended.shape, bf16),
        ),
        in_specs=[in_vmem] * 6,
        out_specs=[in_vmem] * 5,
        name="last",
    )(gradient, master_weight, first_moment, second_moment, new_kv, attended)


def solution(mesh):
    in_specs = (
        P(("learn", "dp"), "tp"),
        P(("learn", "dp"), "tp"),
        P(("learn", "dp"), "tp"),
        P(("learn", "dp"), "tp"),
        P(("learn", "dp"), "tp"),
        P(None, ("learn", "dp"), None),
        P(None, ("learn", "dp"), "tp"),
        P(None, ("learn", "dp"), "tp", None, None),
        P(("learn", "dp")),
    )
    out_specs = (
        P(("learn", "dp"), "tp"),
        P(("learn", "dp"), "tp"),
        P(("learn", "dp"), "tp"),
        P(None, ("learn", "dp"), "tp"),
        P(None, ("learn", "dp"), "tp"),
    )
    return jax.shard_map(shards, mesh=mesh, in_specs=in_specs, out_specs=out_specs, check_vma=False)
```

time: 88.3 us -> 82.4 us (0.933)
  local copies, waits for them, and re-layouts: 2.71 us -> 0 us
  other arithmetic: 1.95 us -> 0 us
  Pallas kernels: 81.8 us -> 80.6 us
    pallas_call x1, Pallas kernels: 81.8 us -> 78.4 us  [shards(): pl.pallas_call(functools.partial(kernel, tuple(shapes)), out_shape=(jax.S...]
    unnamed x8 -> x0, local copies, waits for them, and re-layouts: 2.71 us -> none
    pallas_call x0 -> x1, Pallas kernels: none -> 2.25 us  [shards(): pl.pallas_call(last, out_shape=(like, like, like, jax.ShapeDtypeStruct(ne...]
    sub x1 -> x0, other arithmetic: 1.95 us -> none  [adam(): return (master - learn_rate * (update + decay_rate * master), first, second)]
where the time goes in v3:
time: 82.4 us; the launch traced here: 81.3 us
  Pallas kernels  80.6 us (98%)
    pallas_call x1, Pallas kernels, shards(): pl.pallas_call(functools.partial(kernel, tuple(shapes)), out_shape=(jax.S...  78.4 us
    pallas_call x1, Pallas kernels, shards(): pl.pallas_call(last, out_shape=(like, like, like, jax.ShapeDtypeStruct(ne...  2.25 us

profile of v3, /device:TPU:18, one launch (start us, length us, event | category | flops | bytes accessed | tf_op | source)
XLA Modules:
  0.0 81.3 jit_solution(9268213990711901951)
XLA Ops:
  0.6 78.4 %fused_step.1 = (f32[128,512]{1,0:T(8,128)}, bf16[4,2,512]{2,1,0:T(2,128)(2,1)}, bf16[4,2,2048]{2,1,0:T(2,128)(2,1)}) custom-call(s32[2]{0:T(128)} %refs_0_.1, bf16[4,2,2048]{2,1,0:T(2,128)(2,1)} %refs_1_.1, bf16[4,2,8192]{2,1,0:T(2,128)(2,1)} %refs_2_.1, bf16[512,2048]{1,0:T(8,128)(2,1)} %refs_3_.1, bf16[512,512]{1,0:T(8,128)(2,1)} %refs_4_.1, ...), custom_call_target="tpu_custom_call" | custom-call | tf_op jit(solution)/shard_map/fused_step/pallas_call | solution.py:810
  79.0 2.2 %last.1 = (f32[128,512]{1,0:T(8,128)}, f32[128,512]{1,0:T(8,128)}, f32[128,512]{1,0:T(8,128)}, bf16[4,2,512]{2,1,0:T(2,128)(2,1)}, bf16[4,2,2048]{2,1,0:T(2,128)(2,1)}) custom-call(f32[128,512]{1,0:T(8,128)} %get-tuple-element.8.gradient, f32[128,512]{1,0:T(8,128)} %master.1, f32[128,512]{1,0:T(8,128)} %first.1, f32[128,512]{1,0:T(8,128)} %second.1, ...), custom_call_target="tpu_custom_call" | custom-call | tf_op jit(solution)/shard_map/last/pallas_call | solution.py:836

commit v4 on v3

--- a/solution.py
+++ b/solution.py
@@ -17,15 +17,15 @@
 UNITS = 8
 NX, NY, NZ = 4, 4, 8
 NEW = 'P'
-PLACES = ((0, 0), (0, 1), (1, 0), (3, 0), (2, 0), (1, 1), (3, 1), (2, 1))
-Z_UNITS = (1, 3, 6, 7)
+PLACES = ((0, 0), (0, 1), (1, 0), (3, 0), (1, 1), (3, 1), (2, 0), (2, 1))
+Z_UNITS = (1, 2, 4, 6, 7)
 ORDER = (
-    "B0", "B1", "X0", "C0", "D0", "C1", "D1", "Y0", "A0", "F0", "B2", "E0",
-    "I1", "B3", "C2", "A1", "G0", "F1", "D2", "B5", "J1", "B6", "C3", "D3",
-    "C5", "D5", "C6", "E2", "H0", "K1", "D6", "B4", "B7", "I3", "C4", "E5",
-    "A2", "G2", "L1", "D4", "C7", "J3", "I6", "D7", "A3", "G5", "H2", "E4",
-    "K3", "I7", "J6", "G4", "H5", "J7", "K6", "L3", "K7", "H4", "L6", "P0",
-    "L7", "Q0", "P1", "Q1", "R0", "R1", "S0", "S1",
+    "B0", "B1", "X0", "C0", "D0", "C1", "D1", "Y0", "A0", "F0", "B2", "B3",
+    "E0", "C2", "A1", "I1", "D2", "C3", "F1", "G0", "B4", "B5", "D3", "C4",
+    "J1", "A2", "I2", "D4", "B6", "C5", "D5", "C6", "E3", "K1", "B7", "H0",
+    "D6", "J2", "C7", "I4", "A3", "D7", "E5", "L1", "G3", "K2", "I6", "J4",
+    "I7", "G5", "J6", "K4", "J7", "H3", "K6", "L2", "K7", "H5", "L4", "L6",
+    "L7", "P0", "P1", "Q0", "Q1", "R0", "R1", "S0", "S1",
 )
 
 bf16 = jnp.bfloat16
@@ -74,25 +74,25 @@
         x1_recv=pltpu.VMEM((UNITS, 2, 2, 4, part, half), bf16),
         x2_send=pltpu.VMEM((UNITS, 2, 4, part, half), bf16),
         x2_recv=pltpu.VMEM((UNITS, 2, 4, part, half), bf16),
-        a_send=pltpu.VMEM((len(Z_UNITS), 2, 2, 4, part, half), bf16),
-        a_recv=pltpu.VMEM((len(Z_UNITS), 2, 2, 4, part, half), bf16),
-        a_keep=pltpu.VMEM((len(Z_UNITS), 2, 2, 4, part, half), f32),
-        b_keep=pltpu.VMEM((len(Z_UNITS), 2, 2, 2, part, half), f32),
-        b_send=pltpu.VMEM((len(Z_UNITS), 2, 2, 2, part, half), bf16),
-        b_recv=pltpu.VMEM((len(Z_UNITS), 2, 2, 2, part, half), bf16),
-        c_send=pltpu.VMEM((len(Z_UNITS), 2, 2, part, half), bf16),
-        c_recv=pltpu.VMEM((len(Z_UNITS), 2, 2, part, half), bf16),
+        a_send=pltpu.VMEM((max(1, len(Z_UNITS)), 2, 2, 4, part, half), bf16),
+        a_recv=pltpu.VMEM((max(1, len(Z_UNITS)), 2, 2, 4, part, half), bf16),
+        a_keep=pltpu.VMEM((max(1, len(Z_UNITS)), 2, 2, 4, part, half), f32),
+        b_keep=pltpu.VMEM((max(1, len(Z_UNITS)), 2, 2, 2, part, half), f32),
+        b_send=pltpu.VMEM((max(1, len(Z_UNITS)), 2, 2, 2, part, half), bf16),
+        b_recv=pltpu.VMEM((max(1, len(Z_UNITS)), 2, 2, 2, part, half), bf16),
+        c_send=pltpu.VMEM((max(1, len(Z_UNITS)), 2, 2, part, half), bf16),
+        c_recv=pltpu.VMEM((max(1, len(Z_UNITS)), 2, 2, part, half), bf16),
         d_sum=pltpu.VMEM((4, part, half), f32),
-        d_send=pltpu.VMEM((len(Z_UNITS), 3, part, half), bf16),
-        d_recv=pltpu.VMEM((len(Z_UNITS), 3, part, half), bf16),
-        a_ss=dma((len(Z_UNITS), 2)),
-        a_rs=dma((len(Z_UNITS), 2)),
-        b_ss=dma((len(Z_UNITS), 2)),
-        b_rs=dma((len(Z_UNITS), 2)),
-        c_ss=dma((len(Z_UNITS), 2)),
-        c_rs=dma((len(Z_UNITS), 2)),
-        d_ss=dma((len(Z_UNITS),)),
-        d_rs=dma((len(Z_UNITS),)),
+        d_send=pltpu.VMEM((max(1, len(Z_UNITS)), 3, part, half), bf16),
+        d_recv=pltpu.VMEM((max(1, len(Z_UNITS)), 3, part, half), bf16),
+        a_ss=dma((max(1, len(Z_UNITS)), 2)),
+        a_rs=dma((max(1, len(Z_UNITS)), 2)),
+        b_ss=dma((max(1, len(Z_UNITS)), 2)),
+        b_rs=dma((max(1, len(Z_UNITS)), 2)),
+        c_ss=dma((max(1, len(Z_UNITS)), 2)),
+        c_rs=dma((max(1, len(Z_UNITS)), 2)),
+        d_ss=dma((max(1, len(Z_UNITS)),)),
+        d_rs=dma((max(1, len(Z_UNITS)),)),
         z_sum=pltpu.VMEM((NZ, part, half), f32),
         z_own=pltpu.VMEM((UNITS, part, half), f32),
         z_send=pltpu.VMEM((UNITS, NZ - 1, part, half), bf16),
@@ -102,6 +102,8 @@
         kv=pltpu.VMEM((2, 2, 2, slots, head), bf16),
         state=pltpu.VMEM((3, rows, columns), f32),
         rollout=pltpu.VMEM((rows, columns), bf16),
+        q_in=pltpu.VMEM((4, 2, 16 * head), bf16),
+        x_in=pltpu.VMEM((4, 2, 64 * rows), bf16),
         x_mine=pltpu.VMEM((2, 32, 8, rows), f32),
         x_pair=pltpu.VMEM((32, 8, rows), f32),
         xz_send=pltpu.VMEM((NZ - 1, NX, 16, rows), bf16),
@@ -122,7 +124,7 @@
         att=pltpu.VMEM((2, 64, head), f32),
         top=pltpu.VMEM((2, 64, head), f32),
         total=pltpu.VMEM((2, 64, head), f32),
-        load_sem=dma((7,)),
+        load_sem=dma((9,)),
         out_sem=dma((2, 4)),
         cot_ss=dma((6,)),
         cot_rs=dma((UNITS,)),
@@ -149,7 +151,7 @@
 
 
 def kernel(names, *refs):
-    (lengths, q_ref, x_ref, f_hbm, c_hbm, w_hbm, m_hbm, v_hbm, kv_hbm) = refs[:9]
+    (lengths, q_hbm, x_hbm, f_hbm, c_hbm, w_hbm, m_hbm, v_hbm, kv_hbm) = refs[:9]
     (grad_out, new_out, att_out) = refs[9:12]
     r = types.SimpleNamespace(**dict(zip(names, refs[12:])))
     x, y, z, core = position()
@@ -173,15 +175,13 @@
                 (w_hbm, r.state.at[0]),
                 (m_hbm, r.state.at[1]),
                 (v_hbm, r.state.at[2]),
+                (q_hbm, r.q_in),
+                (x_hbm, r.x_in),
             )
         )
     ]
-    for load in loads[:3]:
-        load.start()
-
-    inputs = jnp.concatenate([x_ref[s].astype(f32) for s in range(4)], axis=0)
-    for block in range(64):
-        r.x_mine[block % 2, block // 2] = inputs[:, block * rows : (block + 1) * rows]
+    for index in (1, 0, 2, 8):
+        loads[index].start()
 
     barrier = pltpu.get_barrier_semaphore()
 
@@ -209,15 +209,16 @@
     pl.semaphore_wait(barrier, 1 + (NX - 1) + (NZ - 1) + (NY - 1) + 8 - 2 * same)
 
     slot = {place: unit for unit, place in enumerate(PLACES)}
-    arrived = {slot[0, 0], slot[0, 1]}
+    arrived = {slot[0, 0]}
 
     def cot_copy(index):
         step = (3, 1, 3, 1, 1, 3)[index]
         half_of = (0, 0, 1, 1, 0, 1)[index]
         source = slot[0, half_of] if index < 4 else slot[(3, 1)[half_of], half_of]
         target = slot[4 - step, half_of] if index < 4 else slot[2, half_of]
-        return send(
-            r.cot.at[source],
+        start = c_hbm.at[:, pl.ds(half_of * half, half)] if index < 4 else r.cot.at[source]
+        return send(
+            start,
             r.cot.at[target],
             r.cot_ss.at[index],
             r.cot_rs.at[target],
@@ -225,8 +226,9 @@
         )
 
     def have(unit):
-        if unit not in arrived:
-            arrived.add(unit)
+        if unit == slot[0, 1] and unit not in arrived:
+            loads[2].wait()
+        elif unit not in arrived:
             send(
                 r.cot.at[unit],
                 r.cot.at[unit],
@@ -234,6 +236,7 @@
                 r.cot_rs.at[unit],
                 device(x, (y + 1) % NY, z, core),
             ).wait_recv()
+        arrived.add(unit)
 
     def forward(part_of):
         have(slot[(3, 1)[part_of], part_of])
@@ -246,16 +249,17 @@
         r.xc_sem.at[1],
         device(x, y, z, other),
     )
+    for index in range(4):
+        cot_copy(index).start()
+    loads[8].wait()
+    inputs = jnp.concatenate([r.x_in[s].astype(f32) for s in range(4)], axis=0)
+    for block in range(64):
+        r.x_mine[block % 2, block // 2] = inputs[:, block * rows : (block + 1) * rows]
     x_swap.start()
     loads[0].wait()
-    for index in range(2):
-        cot_copy(index).start()
-    loads[2].wait()
-    for index in range(2, 4):
-        cot_copy(index).start()
     loads[1].wait()
-    for load in loads[3:]:
-        load.start()
+    for index in range(3, 8):
+        loads[index].start()
 
     def turn(side):
         for row_block in range(NZ):
@@ -584,7 +588,8 @@
         row, kv_head = pair // 2, pair % 2
         if pair == 0:
             loads[3].wait()
-            asked = jnp.concatenate([q_ref[s].astype(f32) for s in range(4)], axis=0)
+            loads[7].wait()
+            asked = jnp.concatenate([r.q_in[s].astype(f32) for s in range(4)], axis=0)
             for h in range(2):
                 for g in range(8):
                     r.query[h, :, g, :] = asked[:, (h * 8 + g) * head : (h * 8 + g + 1) * head]
@@ -814,7 +819,7 @@
             jax.ShapeDtypeStruct((steps, own_rows, columns), bf16),
             jax.ShapeDtypeStruct(queries.shape, bf16),
         ),
-        in_specs=[pl.BlockSpec(memory_space=pltpu.SMEM), in_vmem, in_vmem] + [anywhere] * 6,
+        in_specs=[pl.BlockSpec(memory_space=pltpu.SMEM)] + [anywhere] * 8,
         out_specs=(anywhere, in_vmem, in_vmem),
         scratch_shapes=list(shapes.values()),
         compiler_params=pltpu.CompilerParams(

time: 82.4 us -> 79.1 us (0.960)
  Pallas kernels: 80.6 us -> 77.9 us
    pallas_call x1, Pallas kernels: 78.4 us -> 75.7 us  [shards(): pl.pallas_call(functools.partial(kernel, tuple(shapes)), out_shape=(jax.S...]
where the time goes in v4:
time: 79.1 us; the launch traced here: 78.6 us
  Pallas kernels  77.9 us (98%)
    pallas_call x1, Pallas kernels, shards(): pl.pallas_call(functools.partial(kernel, tuple(shapes)), out_shape=(jax.S...  75.7 us
    pallas_call x1, Pallas kernels, shards(): pl.pallas_call(last, out_shape=(like, like, like, jax.ShapeDtypeStruct(ne...  2.25 us

profile of v4, /device:TPU:18, one launch (start us, length us, event | category | flops | bytes accessed | tf_op | source)
XLA Modules:
  0.0 78.6 jit_solution(473635156304743784)
XLA Ops:
  0.6 75.7 %fused_step.1 = (f32[128,512]{1,0:T(8,128)}, bf16[4,2,512]{2,1,0:T(2,128)(2,1)}, bf16[4,2,2048]{2,1,0:T(2,128)(2,1)}) custom-call(s32[2]{0:T(128)} %refs_0_.1, bf16[4,2,2048]{2,1,0:T(2,128)(2,1)} %refs_1_.1, bf16[4,2,8192]{2,1,0:T(2,128)(2,1)} %refs_2_.1, bf16[512,2048]{1,0:T(8,128)(2,1)} %refs_3_.1, bf16[512,512]{1,0:T(8,128)(2,1)} %refs_4_.1, ...), custom_call_target="tpu_custom_call" | custom-call | tf_op jit(solution)/shard_map/fused_step/pallas_call | solution.py:815
  76.3 2.2 %last.1 = (f32[128,512]{1,0:T(8,128)}, f32[128,512]{1,0:T(8,128)}, f32[128,512]{1,0:T(8,128)}, bf16[4,2,512]{2,1,0:T(2,128)(2,1)}, bf16[4,2,2048]{2,1,0:T(2,128)(2,1)}) custom-call(f32[128,512]{1,0:T(8,128)} %get-tuple-element.8.gradient, f32[128,512]{1,0:T(8,128)} %master.1, f32[128,512]{1,0:T(8,128)} %first.1, f32[128,512]{1,0:T(8,128)} %second.1, ...), custom_call_target="tpu_custom_call" | custom-call | tf_op jit(solution)/shard_map/last/pallas_call | solution.py:841

commit v5 on v4

--- a/solution.py
+++ b/solution.py
@@ -273,7 +273,7 @@
             store(i, product.reshape(2, 4, part, half))
             return carry
 
-        lax.fori_loop(0, NZ // 2, step, 0)
+        lax.fori_loop(0, NZ // 2, step, 0, unroll=True)
 
     def core_copy(unit):
         return send(

time: 79.1 us -> 78.5 us (level)
  no operation moved by 1% of the time
where the time goes in v5:
time: 78.5 us; the launch traced here: 78.4 us
  Pallas kernels  77.7 us (99%)
    pallas_call x1, Pallas kernels, shards(): pl.pallas_call(functools.partial(kernel, tuple(shapes)), out_shape=(jax.S...  75.5 us
    pallas_call x1, Pallas kernels, shards(): pl.pallas_call(last, out_shape=(like, like, like, jax.ShapeDtypeStruct(ne...  2.25 us

profile of v5, /device:TPU:18, one launch (start us, length us, event | category | flops | bytes accessed | tf_op | source)
XLA Modules:
  0.0 78.4 jit_solution(6724810627334578594)
XLA Ops:
  0.6 75.5 %fused_step.1 = (f32[128,512]{1,0:T(8,128)}, bf16[4,2,512]{2,1,0:T(2,128)(2,1)}, bf16[4,2,2048]{2,1,0:T(2,128)(2,1)}) custom-call(s32[2]{0:T(128)} %refs_0_.1, bf16[4,2,2048]{2,1,0:T(2,128)(2,1)} %refs_1_.1, bf16[4,2,8192]{2,1,0:T(2,128)(2,1)} %refs_2_.1, bf16[512,2048]{1,0:T(8,128)(2,1)} %refs_3_.1, bf16[512,512]{1,0:T(8,128)(2,1)} %refs_4_.1, ...), custom_call_target="tpu_custom_call" | custom-call | tf_op jit(solution)/shard_map/fused_step/pallas_call | solution.py:815
  76.1 2.2 %last.1 = (f32[128,512]{1,0:T(8,128)}, f32[128,512]{1,0:T(8,128)}, f32[128,512]{1,0:T(8,128)}, bf16[4,2,512]{2,1,0:T(2,128)(2,1)}, bf16[4,2,2048]{2,1,0:T(2,128)(2,1)}) custom-call(f32[128,512]{1,0:T(8,128)} %get-tuple-element.8.gradient, f32[128,512]{1,0:T(8,128)} %master.1, f32[128,512]{1,0:T(8,128)} %first.1, f32[128,512]{1,0:T(8,128)} %second.1, ...), custom_call_target="tpu_custom_call" | custom-call | tf_op jit(solution)/shard_map/last/pallas_call | solution.py:841

commit v6 on v5

--- a/solution.py
+++ b/solution.py
@@ -16,7 +16,6 @@
 MESH = pl.DeviceIdType.MESH
 UNITS = 8
 NX, NY, NZ = 4, 4, 8
-NEW = 'P'
 PLACES = ((0, 0), (0, 1), (1, 0), (3, 0), (1, 1), (3, 1), (2, 0), (2, 1))
 Z_UNITS = (1, 2, 4, 6, 7)
 ORDER = (
@@ -668,8 +667,6 @@
         )
 
     def new0(which):
-        if which == first_head:
-            spread_done()
         for s in range(4):
 
             @pl.when(jnp.logical_or(x != y, x != s))
@@ -772,20 +769,25 @@
         S=new3,
     )
     order = [(word[0], int(word[1])) for word in ORDER]
-    first_head = [place for name, place in order if name == NEW][0]
     turn(other)
-    for name, place in order:
+    def settle():
+        for unit in range(UNITS):
+            if PLACES[unit][0] == 0:
+                pl.when(x != y)(lambda: t_copy(unit).wait_send())
+            else:
+                t_copy(unit).wait_send()
+        for index in range(6):
+            cot_copy(index).wait_send()
+        for which in range(2):
+            for s in range(4):
+                store_copy(which, s).wait()
+
+    for i, (name, place) in enumerate(order):
+        if i == len(order) - 2:
+            settle()
         steps[name](place)
-    for unit in range(UNITS):
-        if PLACES[unit][0] == 0:
-            pl.when(x != y)(lambda: t_copy(unit).wait_send())
-        else:
-            t_copy(unit).wait_send()
-    for index in range(6):
-        cot_copy(index).wait_send()
-    for which in range(2):
-        for s in range(4):
-            store_copy(which, s).wait()
+        if (name, place) == ('A', 3):
+            spread_done()
 
 
 def last(gradient, master, first, second, new_kv, attended, *results):

time: 78.5 us -> 78.4 us (level)
  no operation moved by 1% of the time
where the time goes in v6:
time: 78.4 us; the launch traced here: 78.3 us
  Pallas kernels  77.7 us (99%)
    pallas_call x1, Pallas kernels, shards(): pl.pallas_call(functools.partial(kernel, tuple(shapes)), out_shape=(jax.S...  75.4 us
    pallas_call x1, Pallas kernels, shards(): pl.pallas_call(last, out_shape=(like, like, like, jax.ShapeDtypeStruct(ne...  2.25 us

profile of v6, /device:TPU:18, one launch (start us, length us, event | category | flops | bytes accessed | tf_op | source)
XLA Modules:
  0.0 78.3 jit_solution(14584847806781616501)
XLA Ops:
  0.6 75.4 %fused_step.1 = (f32[128,512]{1,0:T(8,128)}, bf16[4,2,512]{2,1,0:T(2,128)(2,1)}, bf16[4,2,2048]{2,1,0:T(2,128)(2,1)}) custom-call(s32[2]{0:T(128)} %refs_0_.1, bf16[4,2,2048]{2,1,0:T(2,128)(2,1)} %refs_1_.1, bf16[4,2,8192]{2,1,0:T(2,128)(2,1)} %refs_2_.1, bf16[512,2048]{1,0:T(8,128)(2,1)} %refs_3_.1, bf16[512,512]{1,0:T(8,128)(2,1)} %refs_4_.1, ...), custom_call_target="tpu_custom_call" | custom-call | tf_op jit(solution)/shard_map/fused_step/pallas_call | solution.py:817
  76.1 2.2 %last.1 = (f32[128,512]{1,0:T(8,128)}, f32[128,512]{1,0:T(8,128)}, f32[128,512]{1,0:T(8,128)}, bf16[4,2,512]{2,1,0:T(2,128)(2,1)}, bf16[4,2,2048]{2,1,0:T(2,128)(2,1)}) custom-call(f32[128,512]{1,0:T(8,128)} %get-tuple-element.8.gradient, f32[128,512]{1,0:T(8,128)} %master.1, f32[128,512]{1,0:T(8,128)} %first.1, f32[128,512]{1,0:T(8,128)} %second.1, ...), custom_call_target="tpu_custom_call" | custom-call | tf_op jit(solution)/shard_map/last/pallas_call | solution.py:843
